TPU v7x, 512 devices: a whole 4x4x16 slice. The times are simulated.
512 devices in a mesh: dp: 128 (over y, x_lo, z), expert: 4 (over x_hi, core).
Axes of the slice: x: 4 (x_hi: 2, x_lo: 2; x = x_hi * 2 + x_lo), y: 4, z: 16, core: 2. Of those that a mesh axis runs over, the one named last changes fastest.
Arguments:
- tokens: bfloat16 [384, 3072], P('dp', 'expert'), may hold values from -6 to 6
- out_grad: bfloat16 [384, 3072], P('dp', 'expert'), may hold values from -6 to 6
- expert_ids: int32 [384, 2], P('dp'), may hold values from 0 to 3, all different within a row; in each aligned block of 3 rows (0 to 2, 3 to 5, ...) at most 2 rows name the same one
- gate_weights: float32 [384, 2], P('dp'), may hold values from 0.1 to 1
- w_gate: bfloat16 [4, 3072, 16384], P('expert', None, 'dp'), may hold values from -0.109375 to 0.109375
- w_up: bfloat16 [4, 3072, 16384], P('expert', None, 'dp'), may hold values from -0.109375 to 0.109375
- w_down: bfloat16 [4, 16384, 3072], P('expert', 'dp'), may hold values from -0.046875 to 0.046875
Outputs:
- grad_tokens: bfloat16 [384, 3072], P('dp', 'expert')
- grad_gate: bfloat16 [4, 3072, 16384], P('expert', None, 'dp')
- grad_up: bfloat16 [4, 3072, 16384], P('expert', None, 'dp')
- grad_down: bfloat16 [4, 16384, 3072], P('expert', 'dp')
Inputs may be any that keep to these rules, and one draw needn't show every extreme that they name: `expert_ids`: each token names two different experts. Among the 3 tokens of one index of dp (aligned blocks of rows) no expert is named more than 2 times.
All inputs are finite; a program needn't handle non-finite values.
Results may differ from a plain program's by a relative error of at most 0.0057.
Values may be sent and summed in bfloat16 or wider, within the bound.
A program may use at most 64 MiB of HBM per device.

v0:
```python
import jax
import jax.numpy as jnp
from jax import lax
from jax.sharding import PartitionSpec as P

CAP = 2


def route_table(block_ids, n_expert, capacity):
    flat_ids = block_ids.reshape(-1)
    hits = (flat_ids[:, None] == jnp.arange(n_expert, dtype=jnp.int32)[None, :]).astype(jnp.int32)
    ranks = jnp.sum((jnp.cumsum(hits, axis=0) - hits) * hits, axis=1)
    places = jnp.arange(capacity, dtype=jnp.int32)
    table = hits.T[:, None, :] * (ranks[None, None, :] == places[None, :, None]).astype(jnp.int32)
    return table.astype(jnp.bfloat16)


def contract_rows(left, right):
    return lax.dot_general(
        left, right, (((0,), (0,)), ((), ())), preferred_element_type=jnp.float32
    )


def contract_last(left, right):
    return lax.dot_general(
        left, right, (((1,), (1,)), ((), ())), preferred_element_type=jnp.float32
    )


def shards(tokens, out_grad, expert_ids, gate_weights, w_gate, w_up, w_down):
    n_expert = lax.axis_size("expert")
    tok_count = tokens.shape[0]
    quarter = tokens.shape[1]
    slot_x = jnp.repeat(tokens, 2, axis=0)
    slot_dy = (
        gate_weights.reshape(-1, 1) * jnp.repeat(out_grad, 2, axis=0).astype(jnp.float32)
    ).astype(jnp.bfloat16)
    table = route_table(expert_ids, n_expert, CAP)
    send_x = jnp.einsum("ecs,sd->ecd", table, slot_x, preferred_element_type=jnp.float32).astype(
        jnp.bfloat16
    )
    send_dy = jnp.einsum("ecs,sd->ecd", table, slot_dy, preferred_element_type=jnp.float32).astype(
        jnp.bfloat16
    )
    recv_x, recv_dy = (
        lax.all_to_all(send_x, "expert", split_axis=0, concat_axis=2, tiled=True),
        lax.all_to_all(send_dy, "expert", split_axis=0, concat_axis=2, tiled=True),
    )
    rows_x, rows_dy = (
        lax.all_gather(recv_x, "dp", axis=1, tiled=True),
        lax.all_gather(recv_dy, "dp", axis=1, tiled=True),
    )
    rows_x = rows_x[0]
    rows_dy = rows_dy[0]
    gate_panel = w_gate[0]
    up_panel = w_up[0]
    down_panel = w_down[0]
    gate = jnp.dot(rows_x, gate_panel, preferred_element_type=jnp.float32)
    upper = jnp.dot(rows_x, up_panel, preferred_element_type=jnp.float32)
    sigma = jax.nn.sigmoid(gate)
    active = gate * sigma
    hidden = (active * upper).astype(jnp.bfloat16)
    grad_down = contract_rows(hidden, rows_dy).astype(jnp.bfloat16)
    dhidden = contract_last(rows_dy, down_panel)
    dgate = (dhidden * upper * (sigma + active * (1.0 - sigma))).astype(jnp.bfloat16)
    dup = (dhidden * active).astype(jnp.bfloat16)
    grad_gate = contract_rows(rows_x, dgate).astype(jnp.bfloat16)
    grad_up = contract_rows(rows_x, dup).astype(jnp.bfloat16)
    mine = lax.psum_scatter(
        contract_last(dgate, gate_panel) + contract_last(dup, up_panel),
        "dp",
        scatter_dimension=0,
        tiled=True,
    )
    back = lax.all_to_all(mine[None], "expert", split_axis=2, concat_axis=0, tiled=True)
    slot_sum = jnp.einsum(
        "ecs,ecd->sd", table.astype(jnp.float32), back, precision=lax.Precision.HIGHEST
    )
    grad_x = slot_sum.reshape(tok_count, 2, quarter).sum(axis=1)
    return (grad_x.astype(jnp.bfloat16), grad_gate[None], grad_up[None], grad_down[None])


def solution(mesh):
    placed = (
        P("dp", "expert"),
        P("dp", "expert"),
        P("dp", None),
        P("dp", None),
        P("expert", None, "dp"),
        P("expert", None, "dp"),
        P("expert", "dp", None),
    )
    return jax.shard_map(
        shards,
        mesh=mesh,
        in_specs=placed,
        out_specs=(
            P("dp", "expert"),
            P("expert", None, "dp"),
            P("expert", None, "dp"),
            P("expert", "dp", None),
        ),
        check_vma=False,
    )
```

profile of v0, /device:TPU:1, one launch (start us, length us, event | category | flops | bytes accessed | tf_op | source)
XLA Modules:
  0.0 2453.0 jit_solution(12381189569409929181)
XLA Ops:
  7.2 0.0 copy-start
  7.2 0.0 all-gather.5.cloned.1.call-start
  7.2 0.8 copy.33
  8.1 0.1 eq.65
  8.2 0.2 reduce_window_sum.11
  8.4 0.7 broadcast_in_dim.23
  9.1 0.1 convolution_convert_fusion.3
  9.2 13.8 all_to_all.54
  23.1 0.6 copy.39
  23.7 0.0 all-gather.5.cloned.1.call-update
  23.7 0.0 all-gather.3.cloned.1.call-start
  23.8 0.8 copy.35
  24.5 0.1 mul.59
  24.6 0.7 broadcast_in_dim.22
  25.4 0.2 convolution_convert_fusion.4
  25.6 7.7 all_to_all.55
  33.2 0.6 copy.37
  33.9 0.0 all-gather.3.cloned.1.call-update
  33.9 0.0 all-reduce.3.cloned.1.call-start
  33.9 494.6 %all-gather.5.cloned.1.call-done = bf16[1,256,3072]{2,0,1:T(2,128)(2,1)} async-done(((bf16[1,2,3072]{2,0,1:T(2,128)(2,1)}), bf16[1,256,3072]{2,0,1:T(2,128)(2,1)}) %all-gather.5.cloned.1.call-update) | async-done | bytes 1572880 | tf_op jit(solution)/shard_map/all_gather | solution.py:50
  528.5 2.4 copy.45
  530.9 0.0 copy-done
  530.9 0.0 copy-start.1
  530.9 0.6 fusion.5
  531.5 0.6 copy-done.1
  532.1 0.6 fusion.7
  532.6 582.8 %all-gather.3.cloned.1.call-done = bf16[1,256,3072]{2,0,1:T(2,128)(2,1)} async-done(((bf16[1,2,3072]{2,0,1:T(2,128)(2,1)}), bf16[1,256,3072]{2,0,1:T(2,128)(2,1)}) %all-gather.3.cloned.1.call-update) | async-done | bytes 1572880 | tf_op jit(solution)/shard_map/all_gather | solution.py:51
  1115.4 2.7 multiply_convert_fusion.1
  1118.1 0.6 fusion.13
  1118.7 2.3 convolution_add_fusion
  1121.0 0.0 copy-start.2
  1121.0 0.0 all-reduce.3.cloned.1.call-update
  1121.0 0.1 eq.69
  1121.1 0.1 copy.34
  1121.2 1.3 dynamic-slice
  1123.1 0.0 copy-done.2
  1123.1 0.1 fusion.28
  1123.2 1.5 fusion.1
  1124.7 3.5 fusion.2
  1128.2 1188.6 %all-reduce.3.cloned.1.call-done = f32[256,3072]{1,0:T(8,128)} async-done(((f32[256,3072]{1,0:T(8,128)}), f32[256,3072]{1,0:T(8,128)}) %all-reduce.3.cloned.1.call-update) | async-done | bytes 3145744
  2316.8 0.9 dynamic-slice_bitcast_fusion
  2317.7 2.8 copy.40
  2320.5 0.5 broadcast.58
  2321.0 15.9 reduce
  2336.9 3.0 reshape.85
  2339.9 97.4 %all-to-all-start.2 = ((f32[4,1,1536]{2,1,0:T(1,128)}), f32[4,1,1536]{2,1,0:T(1,128)S(1)}, u32[]{:S(2)}, u32[]{:S(2)}) async-start(f32[4,1,1536]{2,1,0:T(1,128)} %reshape.85), calls=%async_computation.2 | async-start | bytes 49152 | tf_op jit(solution)/shard_map/all_to_all | solution.py:75
  2437.3 1.5 fusion
  2438.8 3.1 all-to-all-done.2
  2441.9 0.7 reduce.1
  2442.6 2.4 reshape.86
  2445.1 0.5 copy.43
  2445.5 0.9 fusion.12
  (9 shorter events, 0.1 us)
Async XLA Ops:
  7.2 523.7 %copy-start = (bf16[1,3072,128]{2,1,0:T(8,128)(2,1)S(1)}, bf16[1,3072,128]{2,1,0:T(8,128)(2,1)}, u32[]{:S(2)}) copy-start(bf16[1,3072,128]{2,1,0:T(8,128)(2,1)} %param.11) | copy-start | bytes 2359300
  7.2 521.4 %all-gather.5.cloned.1.call-start = ((), (), s32[]{:S(2)}) async-start(), calls=%async_computation.4 | async-start | bytes 3170304 | tf_op jit(solution)/shard_map/all_gather | solution.py:50
  23.7 1091.7 %all-gather.3.cloned.1.call-start = ((), (), s32[]{:S(2)}) async-start(), calls=%async_computation.3 | async-start | bytes 3170304 | tf_op jit(solution)/shard_map/all_gather | solution.py:51
  33.9 2282.9 %all-reduce.3.cloned.1.call-start = ((), (), s32[]{:S(2)}) async-start(), calls=%async_computation.5 | async-start | bytes 6291456
  530.9 1.1 copy-start.1
  1121.0 2.1 copy-start.2
  2339.9 102.0 %all-to-all-start.2 = ((f32[4,1,1536]{2,1,0:T(1,128)}), f32[4,1,1536]{2,1,0:T(1,128)S(1)}, u32[]{:S(2)}, u32[]{:S(2)}) async-start(f32[4,1,1536]{2,1,0:T(1,128)} %reshape.85), calls=%async_computation.2 | async-start | bytes 49152 | tf_op jit(solution)/shard_map/all_to_all | solution.py:75
Sparse Core Ops, SparseCore 0:
  23.8 504.6 all-gather.4
  531.2 584.1 all-gather.2
  1121.1 1195.6 all-reduce.2
where the time goes:
time: 2450 us
  waiting for transfers between devices  2270 us (93%)
  starting transfers between devices  97.5 us (4%)
    unnamed x4, waiting for transfers between devices  1190 us
    all_gather x1, waiting for transfers between devices, shards(): lax.all_gather(recv_dy, 'dp', axis=1, tiled=True)  583 us
    all_gather x1, waiting for transfers between devices, shards(): lax.all_gather(recv_x, 'dp', axis=1, tiled=True)  495 us
    all_to_all x1, starting transfers between devices, shards(): lax.all_to_all(mine[None], 'expert', split_axis=2, concat_axis=0, tiled=T...  97.4 us
  transfers between devices with their start and end apart: 4, of which 4 were waited for; matrix products, arithmetic and copies ran while one was open for 1% of the time, Pallas kernels for 0%

commit v1 on v0

v1 whole, which is shorter than its diff:
```python
import jax
import jax.numpy as jnp
from jax import lax
from jax.experimental import pallas as pl
from jax.experimental.pallas import tpu as pltpu
from jax.sharding import PartitionSpec as P

MESH = pl.DeviceIdType.MESH
NX, NY, NZ = 4, 4, 16
TOK = 3
QF = 768
NQ = 4
HALF = QF // 2
GROUP = NZ * TOK
NG = 8
ROWS = NG * GROUP
HID = 128
D = NQ * QF
YW = QF + 128
BF, F32 = jnp.bfloat16, jnp.float32


def dot(a, b):
    return jnp.dot(a, b, preferred_element_type=F32)


def kernel(
    tok_ref, dy_ref, ids_ref, gw_ref, wg_hbm, wu_hbm, wd_hbm,
    gx_ref, gg_ref, gu_ref, gd_ref,
    stage, zb, tk, dy, g, wgu, wgut, wd, wdt, acts, dcat, hid, acc, sbuf, rbuf,
    sl1, rl1, sr1, rr1, sl2, rl2, sr2, rr2, sz, rz, zsum,
    w_sem, zs_sem, zr_sem, as_sem, ar_sem, ds_sem, dr_sem, es_sem, er_sem,
    ps_sem, pr_sem, qs_sem, qr_sem, fs_sem, fr_sem,
):
    dp = lax.axis_index("dp")
    ex = lax.axis_index("expert")
    z, xl, y = dp % NZ, (dp // NZ) % 2, dp // (2 * NZ)
    xh, c = ex // 2, ex % 2
    x = xh * 2 + xl

    def dev(px, py, pz, pc):
        return ((py * 2 + px % 2) * NZ + pz, (px // 2) * 2 + pc)

    def at(dx, dy_):
        return dev((x + dx) % NX, (y + dy_) % NY, z, c)

    sibling = dev(x, y, z, 1 - c)

    def zdev(d):
        return dev(x, y, (z + d) % NZ, c)

    def cell(dx, dy_):
        px, py = (x + dx) % NX, (y + dy_) % NY
        return (px // 2) * 2 + c, py * 2 + px % 2

    loads = [
        pltpu.make_async_copy(wg_hbm.at[0], wgu.at[:, pl.ds(0, HID)], w_sem.at[0]),
        pltpu.make_async_copy(wu_hbm.at[0], wgu.at[:, pl.ds(HID, HID)], w_sem.at[1]),
        pltpu.make_async_copy(wd_hbm.at[0], wd, w_sem.at[2]),
    ]
    for copy in loads:
        copy.start()

    barrier = pltpu.get_barrier_semaphore()
    peers = [zdev(d) for d in range(1, NZ)]
    peers += [at(d, 0) for d in range(1, NX)] + [at(0, d) for d in range(1, NY)] + [sibling]
    for peer in peers:
        pl.semaphore_signal(barrier, inc=1, device_id=peer, device_id_type=MESH)

    stage[...] = jnp.zeros_like(stage)
    for i, ref in enumerate((tok_ref, dy_ref)):
        v = ref[...].astype(F32)
        stage[pl.ds(6 * i, TOK), :] = v[:, :HALF]
        stage[pl.ds(6 * i + TOK, TOK), :] = v[:, HALF:]
    lane = lax.broadcasted_iota(jnp.int32, (TOK, 128), 1)
    w = jnp.zeros((TOK, 128), F32)
    for k in range(2):
        w = w + jnp.where(ids_ref[:, k : k + 1] == lane % 4, gw_ref[:, k : k + 1], 0.0)
    hi = w.astype(BF).astype(F32)
    mid = (w - hi).astype(BF).astype(F32)
    low = w - hi - mid
    w = jnp.where(lane < 4, hi, jnp.where(lane < 8, mid, jnp.where(lane < 12, low, 0.0)))
    stage[pl.ds(12, TOK), pl.ds(0, 128)] = w
    zb[z] = stage[...].astype(BF)

    pl.semaphore_wait(barrier, len(peers))

    def remote(src, dst, ssem, rsem, device):
        return pltpu.make_async_remote_copy(
            src_ref=src, dst_ref=dst, send_sem=ssem, recv_sem=rsem, device_id=device, device_id_type=MESH
        )

    sends = []

    def send(src, dst, ssem, rsem, device):
        copy = remote(src, dst, ssem, rsem, device)
        copy.start()
        sends.append(copy)

    for d in range(1, NZ):
        send(zb.at[z], zb.at[z], zs_sem.at[d], zr_sem.at[d], zdev(d))

    for copy in loads:
        copy.wait()
    for q in range(NQ):
        wgut[q] = wgu[pl.ds(q * QF, QF), :].T
        wdt[pl.ds(q * QF, QF), :] = wd[:, pl.ds(q * QF, QF)].T

    for d in range(1, NZ):
        remote(zb.at[(z - d + NZ) % NZ], zb.at[(z - d + NZ) % NZ], zs_sem.at[d], zr_sem.at[d], zdev(d)).wait_recv()

    r = lax.broadcasted_iota(jnp.int32, (5 * GROUP, NZ * 16), 0)
    s = lax.broadcasted_iota(jnp.int32, (5 * GROUP, NZ * 16), 1)
    k = s % 16
    kind = (k * 11) // 32
    pick = ((r == kind * GROUP + (s // 16) * TOK + (k - 3 * kind)) & (k < 15)).astype(F32).astype(BF)
    rows = dot(pick, zb[...].reshape(NZ * 16, HALF)).astype(BF)
    mq, mg = cell(0, 0)
    tk[mq, mg, :, pl.ds(0, HALF)] = rows[0:GROUP]
    tk[mq, mg, :, pl.ds(HALF, HALF)] = rows[GROUP : 2 * GROUP]
    dy[mq, mg, :, pl.ds(0, HALF)] = rows[2 * GROUP : 3 * GROUP]
    dy[mq, mg, :, pl.ds(HALF, HALF)] = rows[3 * GROUP : 4 * GROUP]
    dy[mq, mg, :, pl.ds(QF, 128)] = rows[4 * GROUP : 5 * GROUP, 0:128]

    arrays = ((tk, 0), (dy, 1))

    def off(h, first, second):
        return (first, second) if h == 0 else (second, first)

    def block(h, first, second):
        q_, g_ = cell(*off(h, first, second))
        return arrays[h][0].at[q_, g_]

    def to_sibling(h, first, second):
        ref = block(h, first, second)
        n = first * 4 + second
        send(ref, ref, ds_sem.at[h, n], dr_sem.at[h, n], sibling)

    def spread_second(h, first):
        ref = block(h, first, 0)
        for d in range(1, 4):
            send(ref, ref, as_sem.at[h, 1 + first, d], ar_sem.at[h, 1 + first, d], at(*off(h, 0, d)))
        to_sibling(h, first, 0)

    for h in range(2):
        ref = block(h, 0, 0)
        for d in range(1, 4):
            send(ref, ref, as_sem.at[h, 0, d], ar_sem.at[h, 0, d], at(*off(h, d, 0)))
    for h in range(2):
        spread_second(h, 0)
    for d in (1, 3, 2):
        for h in range(2):
            ref = block(h, 4 - d, 0)
            remote(ref, ref, as_sem.at[h, 0, d], ar_sem.at[h, 0, d], sibling).wait_recv()
            spread_second(h, 4 - d)
    for first in (0, 3, 1, 2):
        for d in (1, 3, 2):
            for h in range(2):
                ref = block(h, first, 4 - d)
                remote(ref, ref, as_sem.at[h, 1 + first, d], ar_sem.at[h, 1 + first, d], sibling).wait_recv()
                to_sibling(h, first, 4 - d)
    for n in range(16):
        for h in range(2):
            px, py = off(h, n // 4, n % 4)
            qx, gy = cell(px, py)
            ref = arrays[h][0].at[qx + 1 - 2 * c, gy]
            remote(ref, ref, ds_sem.at[h, n], dr_sem.at[h, n], sibling).wait_recv()

    route = dy[mq, :, :, pl.ds(QF, 128)].reshape(ROWS, 128).astype(F32)
    route_lane = lax.broadcasted_iota(jnp.int32, (ROWS, 128), 1)
    weight = jnp.sum(jnp.where(route_lane % 4 == ex, route, 0.0), axis=1, keepdims=True)

    for q in range(NQ):
        part = dot(tk[q].reshape(ROWS, QF), wgu[pl.ds(q * QF, QF), :])
        g[q] = (weight * dy[q, :, :, pl.ds(0, QF)].reshape(ROWS, QF).astype(F32)).astype(BF)
        back = dot(g[q], wdt[pl.ds(q * QF, QF), :])
        if q == 0:
            acts[:, pl.ds(0, 2 * HID)] = part
            acts[:, pl.ds(2 * HID, HID)] = back
        else:
            acts[:, pl.ds(0, 2 * HID)] += part
            acts[:, pl.ds(2 * HID, HID)] += back
    gate, up, dh = acts[:, pl.ds(0, HID)], acts[:, pl.ds(HID, HID)], acts[:, pl.ds(2 * HID, HID)]
    sigma = jax.nn.sigmoid(gate)
    active = gate * sigma
    hid[...] = (active * up).astype(BF)
    dcat[:, pl.ds(0, HID)] = (dh * up * (sigma + active * (1.0 - sigma))).astype(BF)
    dcat[:, pl.ds(HID, HID)] = (dh * active).astype(BF)

    for h in range(2):
        sbuf[h] = dot(dcat[...], wgut[2 * h + 1 - c]).astype(BF).reshape(NG, GROUP, QF)
        send(sbuf.at[h], rbuf.at[h], es_sem.at[h], er_sem.at[h], sibling)
    for h in range(2):
        acc[h] = dot(dcat[...], wgut[2 * h + c]).reshape(NG, GROUP, QF)
    for h in range(2):
        remote(sbuf.at[h], rbuf.at[h], es_sem.at[h], er_sem.at[h], sibling).wait_recv()
        acc[h] = acc[h] + rbuf[h].astype(F32)

    sides = ((sl1, rl1, sl2, rl2), (sr1, rr1, sr2, rr2))

    def home(h, first, second):
        px, py = off(h, first, second)
        px, py = (x + px) % NX, (y + py) % NY
        return px // 2, py * 2 + px % 2

    for d in (2, 1, 3):
        for h in range(2):
            s1, r1, _, _ = sides[h]
            for second in range(4):
                a, b = home(h, d, second)
                s1[d, second] = acc[a, b, :, pl.ds(h * HALF, HALF)].astype(BF)
            send(s1.at[d], r1.at[d], ps_sem.at[h, d], pr_sem.at[h, d], at(*off(h, d, 0)))

    for q in range(NQ):
        both = lax.dot_general(
            tk[q].reshape(ROWS, QF), dcat[...], (((0,), (0,)), ((), ())), preferred_element_type=F32
        ).astype(BF)
        gg_ref[0, pl.ds(q * QF, QF), :] = both[:, :HID]
        gu_ref[0, pl.ds(q * QF, QF), :] = both[:, HID:]
    hid_t = hid[...].T
    for q in range(NQ):
        gd_ref[0, :, pl.ds(q * QF, QF)] = dot(hid_t, g[q]).astype(BF)

    for h in range(2):
        s1, r1, s2, r2 = sides[h]
        for d in range(1, 4):
            remote(s1.at[d], r1.at[d], ps_sem.at[h, d], pr_sem.at[h, d], sibling).wait_recv()
        for second in (2, 1, 3, 0):
            a, b = home(h, 0, second)
            total = acc[a, b, :, pl.ds(h * HALF, HALF)]
            for d in range(1, 4):
                total = total + r1[d, second].astype(F32)
            if second == 0:
                acc[a, b, :, pl.ds(h * HALF, HALF)] = total
            else:
                s2[second] = total.astype(BF)
                send(s2.at[second], r2.at[second], qs_sem.at[h, second], qr_sem.at[h, second], at(*off(h, 0, second)))
    a0, b0 = home(0, 0, 0)
    for h in range(2):
        s1, r1, s2, r2 = sides[h]
        total = acc[a0, b0, :, pl.ds(h * HALF, HALF)]
        for d in range(1, 4):
            remote(s2.at[d], r2.at[d], qs_sem.at[h, d], qr_sem.at[h, d], sibling).wait_recv()
            total = total + r2[d].astype(F32)
        zsum[:, pl.ds(h * HALF, HALF)] = total.astype(BF)

    r = lax.broadcasted_iota(jnp.int32, (NZ * 16, GROUP), 0)
    s = lax.broadcasted_iota(jnp.int32, (NZ * 16, GROUP), 1)
    packed = jnp.zeros((NZ * 16, 256), F32)
    for third in range(3):
        k = r % 16 - 3 * third
        place = ((k >= 0) & (k < TOK) & (s == (r // 16) * TOK + k)).astype(F32).astype(BF)
        packed = packed + dot(place, zsum[:, pl.ds(256 * third, 256)])
    sz[...] = packed.astype(BF).reshape(NZ, 16, 256)
    for d in (8, 7, 9, 6, 10, 5, 11, 4, 12, 3, 13, 2, 14, 1, 15):
        send(sz.at[(z + d) % NZ], rz.at[d], fs_sem.at[d], fr_sem.at[d], zdev(d))
    total = sz[z].astype(F32)
    for d in range(1, NZ):
        remote(sz.at[(z + d) % NZ], rz.at[d], fs_sem.at[d], fr_sem.at[d], zdev(d)).wait_recv()
        total = total + rz[d].astype(F32)
    stage[:, pl.ds(0, 256)] = total
    for third in range(3):
        gx_ref[:, pl.ds(256 * third, 256)] = stage[pl.ds(3 * third, TOK), pl.ds(0, 256)].astype(BF)

    for copy in sends:
        copy.wait_send()


def shards(tokens, out_grad, expert_ids, gate_weights, w_gate, w_up, w_down):
    vmem = pl.BlockSpec(memory_space=pltpu.VMEM)
    anywhere = pl.BlockSpec(memory_space=pl.ANY)
    dma = pltpu.SemaphoreType.DMA
    return pl.pallas_call(
        kernel,
        out_shape=(
            jax.ShapeDtypeStruct((TOK, QF), BF),
            jax.ShapeDtypeStruct((1, D, HID), BF),
            jax.ShapeDtypeStruct((1, D, HID), BF),
            jax.ShapeDtypeStruct((1, HID, D), BF),
        ),
        in_specs=[vmem] * 4 + [anywhere] * 3,
        out_specs=(vmem,) * 4,
        scratch_shapes=[
            pltpu.VMEM((16, HALF), F32),
            pltpu.VMEM((NZ, 16, HALF), BF),
            pltpu.VMEM((NQ, NG, GROUP, QF), BF),
            pltpu.VMEM((NQ, NG, GROUP, YW), BF),
            pltpu.VMEM((NQ, ROWS, QF), BF),
            pltpu.VMEM((D, 2 * HID), BF),
            pltpu.VMEM((NQ, 2 * HID, QF), BF),
            pltpu.VMEM((HID, D), BF),
            pltpu.VMEM((D, HID), BF),
            pltpu.VMEM((ROWS, 3 * HID), F32),
            pltpu.VMEM((ROWS, 2 * HID), BF),
            pltpu.VMEM((ROWS, HID), BF),
            pltpu.VMEM((2, NG, GROUP, QF), F32),
            pltpu.VMEM((2, NG, GROUP, QF), BF),
            pltpu.VMEM((2, NG, GROUP, QF), BF),
            pltpu.VMEM((4, 4, GROUP, HALF), BF),
            pltpu.VMEM((4, 4, GROUP, HALF), BF),
            pltpu.VMEM((4, 4, GROUP, HALF), BF),
            pltpu.VMEM((4, 4, GROUP, HALF), BF),
            pltpu.VMEM((4, GROUP, HALF), BF),
            pltpu.VMEM((4, GROUP, HALF), BF),
            pltpu.VMEM((4, GROUP, HALF), BF),
            pltpu.VMEM((4, GROUP, HALF), BF),
            pltpu.VMEM((NZ, 16, 256), BF),
            pltpu.VMEM((NZ, 16, 256), BF),
            pltpu.VMEM((GROUP, QF), BF),
            dma((3,)),
            dma((NZ,)), dma((NZ,)),
            dma((2, 5, 4)), dma((2, 5, 4)),
            dma((2, 16)), dma((2, 16)),
            dma((2,)), dma((2,)),
            dma((2, 4)), dma((2, 4)),
            dma((2, 4)), dma((2, 4)),
            dma((NZ,)), dma((NZ,)),
        ],
        compiler_params=pltpu.CompilerParams(
            collective_id=0, has_side_effects=True, vmem_limit_bytes=48 * 2**20
        ),
        cost_estimate=pl.CostEstimate(flops=2_400_000_000, bytes_accessed=4_800_000, transcendentals=49152),
        name="moe_backward",
    )(tokens, out_grad, expert_ids, gate_weights, w_gate, w_up, w_down)


def solution(mesh):
    placed = (
        P("dp", "expert"),
        P("dp", "expert"),
        P("dp", None),
        P("dp", None),
        P("expert", None, "dp"),
        P("expert", None, "dp"),
        P("expert", "dp", None),
    )
    return jax.shard_map(
        shards,
        mesh=mesh,
        in_specs=placed,
        out_specs=(
            P("dp", "expert"),
            P("expert", None, "dp"),
            P("expert", None, "dp"),
            P("expert", "dp", None),
        ),
        check_vma=False,
    )
```

time: 2450 us -> 86.2 us (0.04)
  waiting for transfers between devices: 2270 us -> 0 us
  starting transfers between devices: 97.5 us -> 0 us
  Pallas kernels: 0 us -> 75.8 us
    unnamed x4 -> x0, waiting for transfers between devices: 1190 us -> none
    all_gather x2 -> x0, waiting for transfers between devices: 1080 us -> none  [the longest x1 583 us: shards(): lax.all_gather(recv_dy, 'dp', axis=1, tiled=True)]
    all_to_all x1 -> x0, starting transfers between devices: 97.4 us -> none  [shards(): lax.all_to_all(mine[None], 'expert', split_axis=2, concat_axis=0, tiled=T...]
    pallas_call x0 -> x1, Pallas kernels: none -> 75.8 us  [shards(): pl.pallas_call(kernel, out_shape=(jax.ShapeDtypeStruct((TOK, QF), BF), ja...]
  transfers between devices with their start and end apart: 4 -> 0, of which waited for: 4 -> 0; matrix products, arithmetic and copies ran while one was open for 1% -> 0% of each run, Pallas kernels for 0% -> 0%
where the time goes in v1:
time: 86.2 us; the launch traced here: 85.3 us
  Pallas kernels  75.8 us (88%)
  local copies, waits for them, and re-layouts  8.86 us (10%)
    pallas_call x1, Pallas kernels, shards(): pl.pallas_call(kernel, out_shape=(jax.ShapeDtypeStruct((TOK, QF), BF), ja...  75.8 us
    unnamed x16, local copies, waits for them, and re-layouts  8.86 us

profile of v1, /device:TPU:1, one launch (start us, length us, event | category | flops | bytes accessed | tf_op | source)
XLA Modules:
  0.0 85.3 jit_solution(5577712490864699240)
XLA Ops:
  0.6 0.0 copy-start.3
  0.6 0.8 copy.11.ids_ref
  1.4 0.8 copy.12.gw_ref
  2.2 0.0 copy-done.3
  2.2 0.0 copy-start
  2.2 1.1 %copy-done = bf16[1,3072,128]{2,1,0:T(8,128)(2,1)S(1)} copy-done((bf16[1,3072,128]{2,1,0:T(8,128)(2,1)S(1)}, bf16[1,3072,128]{2,1,0:T(8,128)(2,1)}, u32[]{:S(2)}) %copy-start) | copy-done | bytes 786456
  3.3 0.0 copy-start.1
  3.3 1.1 %copy-done.1 = bf16[1,3072,128]{2,1,0:T(8,128)(2,1)S(1)} copy-done((bf16[1,3072,128]{2,1,0:T(8,128)(2,1)S(1)}, bf16[1,3072,128]{2,1,0:T(8,128)(2,1)}, u32[]{:S(2)}) %copy-start.1) | copy-done | bytes 786456
  4.4 0.0 copy-start.2
  4.4 1.1 %copy-done.2 = bf16[1,128,3072]{2,1,0:T(8,128)(2,1)S(1)} copy-done((bf16[1,128,3072]{2,1,0:T(8,128)(2,1)S(1)}, bf16[1,128,3072]{2,1,0:T(8,128)(2,1)}, u32[]{:S(2)}) %copy-start.2) | copy-done | bytes 786456
  5.6 0.0 copy-start.4
  5.6 0.7 copy-done.4
  6.3 75.8 %moe_backward.1 = (bf16[3,768]{1,0:T(4,128)(2,1)S(1)}, bf16[1,3072,128]{2,1,0:T(8,128)(2,1)S(1)}, bf16[1,3072,128]{2,1,0:T(8,128)(2,1)S(1)}, bf16[1,128,3072]{2,1,0:T(8,128)(2,1)S(1)}) custom-call(bf16[3,768]{1,0:T(4,128)(2,1)S(1)} %copy-done.3, bf16[3,768]{1,0:T(4,128)(2,1)S(1)} %copy-done.4, s32[3,2]{1,0:T(4,128)S(1)} %copy.11.ids_ref, ...), custom_call_target="tpu_custom_call" | custom-call | flops 2400000000 | bytes 4800000 | tf_op jit(solution)/shard_map/moe_backward/pallas_call | solution.py:273
  82.0 0.6 copy.17
  82.6 0.9 %copy.18 = bf16[1,3072,128]{2,1,0:T(8,128)(2,1)} copy(bf16[1,3072,128]{2,1,0:T(8,128)(2,1)S(1)} %get-tuple-element.9) | data formatting | bytes 1572864
  83.5 0.9 %copy.19 = bf16[1,3072,128]{2,1,0:T(8,128)(2,1)} copy(bf16[1,3072,128]{2,1,0:T(8,128)(2,1)S(1)} %get-tuple-element.10) | data formatting | bytes 1572864
  84.4 0.9 %copy.20 = bf16[1,128,3072]{2,1,0:T(8,128)(2,1)} copy(bf16[1,128,3072]{2,1,0:T(8,128)(2,1)S(1)} %get-tuple-element.11) | data formatting | bytes 1572864
Async XLA Ops:
  0.6 1.5 %copy-start.3 = (bf16[3,768]{1,0:T(4,128)(2,1)S(1)}, bf16[3,768]{1,0:T(4,128)(2,1)}, u32[]{:S(2)}) copy-start(bf16[3,768]{1,0:T(4,128)(2,1)} %tok_ref.1) | copy-start | bytes 13828
  2.2 1.1 %copy-start = (bf16[1,3072,128]{2,1,0:T(8,128)(2,1)S(1)}, bf16[1,3072,128]{2,1,0:T(8,128)(2,1)}, u32[]{:S(2)}) copy-start(bf16[1,3072,128]{2,1,0:T(8,128)(2,1)} %wg_hbm.1) | copy-start | bytes 2359300
  3.3 1.1 %copy-start.1 = (bf16[1,3072,128]{2,1,0:T(8,128)(2,1)S(1)}, bf16[1,3072,128]{2,1,0:T(8,128)(2,1)}, u32[]{:S(2)}) copy-start(bf16[1,3072,128]{2,1,0:T(8,128)(2,1)} %wu_hbm.1) | copy-start | bytes 2359300
  4.4 1.1 %copy-start.2 = (bf16[1,128,3072]{2,1,0:T(8,128)(2,1)S(1)}, bf16[1,128,3072]{2,1,0:T(8,128)(2,1)}, u32[]{:S(2)}) copy-start(bf16[1,128,3072]{2,1,0:T(8,128)(2,1)} %wd_hbm.1) | copy-start | bytes 2359300
  5.6 0.7 copy-start.4

commit v2 on v1

--- a/solution.py
+++ b/solution.py
@@ -7,6 +7,7 @@
 
 MESH = pl.DeviceIdType.MESH
 NX, NY, NZ = 4, 4, 16
+PEERS_Z = (1, 2, 3, 4, -1, -2, -3, -4)
 TOK = 3
 QF = 768
 NQ = 4
@@ -17,6 +18,8 @@
 HID = 128
 D = NQ * QF
 YW = QF + 128
+WIDE = (QF, YW)
+CUT = (384, 512)
 BF, F32 = jnp.bfloat16, jnp.float32
 
 
@@ -26,32 +29,38 @@
 
 def kernel(
     tok_ref, dy_ref, ids_ref, gw_ref, wg_hbm, wu_hbm, wd_hbm,
-    gx_ref, gg_ref, gu_ref, gd_ref,
+    gx_ref, gg_hbm, gu_hbm, gd_hbm,
     stage, zb, tk, dy, g, wgu, wgut, wd, wdt, acts, dcat, hid, acc, sbuf, rbuf,
-    sl1, rl1, sr1, rr1, sl2, rl2, sr2, rr2, sz, rz, zsum,
-    w_sem, zs_sem, zr_sem, as_sem, ar_sem, ds_sem, dr_sem, es_sem, er_sem,
+    sl1, rl1, sr1, rr1, sl2, rl2, sr2, rr2, sz, rz, zsum, gg, gu, gd,
+    w_sem, o_sem, zs_sem, zr_sem, as_sem, ar_sem, ds_sem, dr_sem, es_sem, er_sem,
     ps_sem, pr_sem, qs_sem, qr_sem, fs_sem, fr_sem,
 ):
     dp = lax.axis_index("dp")
     ex = lax.axis_index("expert")
-    z, xl, y = dp % NZ, (dp // NZ) % 2, dp // (2 * NZ)
-    xh, c = ex // 2, ex % 2
+    rem, div = lax.rem, lax.div
+    z, xl, y = rem(dp, NZ), rem(div(dp, NZ), 2), div(dp, 2 * NZ)
+    xh, c = div(ex, 2), rem(ex, 2)
     x = xh * 2 + xl
 
-    def dev(px, py, pz, pc):
-        return ((py * 2 + px % 2) * NZ + pz, (px // 2) * 2 + pc)
+    xs = [x] + [rem(x + d, NX) for d in range(1, NX)]
+    ys = [y] + [rem(y + d, NY) for d in range(1, NY)]
+    zs = [z] + [rem(z + d, NZ) for d in range(1, NZ)]
+    xhs, xls = [div(v, 2) for v in xs], [rem(v, 2) for v in xs]
+    planes = [[(ys[j] * 2 + xls[i], xhs[i] * 2 + c) for j in range(NY)] for i in range(NX)]
+    here = planes[0][0][0] * NZ
+    sibling = (dp, ex + 1 - 2 * c)
+    along_z = [(here + zs[d], ex) for d in range(NZ)]
+    around = {(i, j): (planes[i][j][0] * NZ + z, planes[i][j][1]) for i in range(NX) for j in range(NY) if i * j == 0}
 
     def at(dx, dy_):
-        return dev((x + dx) % NX, (y + dy_) % NY, z, c)
-
-    sibling = dev(x, y, z, 1 - c)
+        return around[dx % NX, dy_ % NY]
 
     def zdev(d):
-        return dev(x, y, (z + d) % NZ, c)
+        return along_z[d % NZ]
 
     def cell(dx, dy_):
-        px, py = (x + dx) % NX, (y + dy_) % NY
-        return (px // 2) * 2 + c, py * 2 + px % 2
+        group, quarter = planes[dx % NX][dy_ % NY]
+        return quarter, group
 
     loads = [
         pltpu.make_async_copy(wg_hbm.at[0], wgu.at[:, pl.ds(0, HID)], w_sem.at[0]),
@@ -62,7 +71,7 @@
         copy.start()
 
     barrier = pltpu.get_barrier_semaphore()
-    peers = [zdev(d) for d in range(1, NZ)]
+    peers = [zdev(d) for d in PEERS_Z]
     peers += [at(d, 0) for d in range(1, NX)] + [at(0, d) for d in range(1, NY)] + [sibling]
     for peer in peers:
         pl.semaphore_signal(barrier, inc=1, device_id=peer, device_id_type=MESH)
@@ -72,15 +81,16 @@
         v = ref[...].astype(F32)
         stage[pl.ds(6 * i, TOK), :] = v[:, :HALF]
         stage[pl.ds(6 * i + TOK, TOK), :] = v[:, HALF:]
-    lane = lax.broadcasted_iota(jnp.int32, (TOK, 128), 1)
-    w = jnp.zeros((TOK, 128), F32)
-    for k in range(2):
-        w = w + jnp.where(ids_ref[:, k : k + 1] == lane % 4, gw_ref[:, k : k + 1], 0.0)
-    hi = w.astype(BF).astype(F32)
-    mid = (w - hi).astype(BF).astype(F32)
-    low = w - hi - mid
-    w = jnp.where(lane < 4, hi, jnp.where(lane < 8, mid, jnp.where(lane < 12, low, 0.0)))
-    stage[pl.ds(12, TOK), pl.ds(0, 128)] = w
+    lane = lax.broadcasted_iota(jnp.int32, (1, 128), 1)
+    for t in range(TOK):
+        w = jnp.zeros((1, 128), F32)
+        for k in range(2):
+            w = w + jnp.where(ids_ref[k, t] == lane % 4, gw_ref[k, t], 0.0)
+        hi = w.astype(BF).astype(F32)
+        mid = (w - hi).astype(BF).astype(F32)
+        low = w - hi - mid
+        w = jnp.where(lane < 4, hi, jnp.where(lane < 8, mid, jnp.where(lane < 12, low, 0.0)))
+        stage[pl.ds(12 + t, 1), pl.ds(0, 128)] = w
     zb[z] = stage[...].astype(BF)
 
     pl.semaphore_wait(barrier, len(peers))
@@ -97,17 +107,31 @@
         copy.start()
         sends.append(copy)
 
-    for d in range(1, NZ):
-        send(zb.at[z], zb.at[z], zs_sem.at[d], zr_sem.at[d], zdev(d))
-
+    def pass_on(origin, step, d):
+        ref = zb.at[zs[origin % NZ]]
+        send(ref, ref, zs_sem.at[d % NZ], zr_sem.at[d % NZ], zdev(step))
+
+    for d in (4, -4, 2, -2, 1, -1):
+        pass_on(0, d, d)
+
+    def arrived(d):
+        ref = zb.at[zs[-d % NZ]]
+        remote(ref, ref, zs_sem.at[d % NZ], zr_sem.at[d % NZ], sibling).wait_recv()
+
+    arrived(4)
+    for step in (4, 3, 2, 1, -1):
+        pass_on(-4, step, 4 + step)
+    arrived(-4)
+    for step in (-3, -2, -1, 1):
+        pass_on(4, step, step - 4)
     for copy in loads:
         copy.wait()
     for q in range(NQ):
         wgut[q] = wgu[pl.ds(q * QF, QF), :].T
         wdt[pl.ds(q * QF, QF), :] = wd[:, pl.ds(q * QF, QF)].T
 
-    for d in range(1, NZ):
-        remote(zb.at[(z - d + NZ) % NZ], zb.at[(z - d + NZ) % NZ], zs_sem.at[d], zr_sem.at[d], zdev(d)).wait_recv()
+    for d in (1, -1, 2, -2, 3, -3, 5, -5, 6, -6, 7, -7, 8):
+        arrived(d)
 
     r = lax.broadcasted_iota(jnp.int32, (5 * GROUP, NZ * 16), 0)
     s = lax.broadcasted_iota(jnp.int32, (5 * GROUP, NZ * 16), 1)
@@ -127,38 +151,71 @@
     def off(h, first, second):
         return (first, second) if h == 0 else (second, first)
 
-    def block(h, first, second):
+    def block(h, first, second, part=None):
         q_, g_ = cell(*off(h, first, second))
-        return arrays[h][0].at[q_, g_]
+        if part is None:
+            return arrays[h][0].at[q_, g_]
+        return arrays[h][0].at[q_, g_, :, pl.ds(*((0, CUT[h]) if part == 0 else (CUT[h], WIDE[h] - CUT[h])))]
 
     def to_sibling(h, first, second):
         ref = block(h, first, second)
-        n = first * 4 + second
+        n = (first % 4) * 4 + second % 4
         send(ref, ref, ds_sem.at[h, n], dr_sem.at[h, n], sibling)
 
-    def spread_second(h, first):
-        ref = block(h, first, 0)
-        for d in range(1, 4):
-            send(ref, ref, as_sem.at[h, 1 + first, d], ar_sem.at[h, 1 + first, d], at(*off(h, 0, d)))
-        to_sibling(h, first, 0)
-
-    for h in range(2):
-        ref = block(h, 0, 0)
-        for d in range(1, 4):
-            send(ref, ref, as_sem.at[h, 0, d], ar_sem.at[h, 0, d], at(*off(h, d, 0)))
-    for h in range(2):
-        spread_second(h, 0)
-    for d in (1, 3, 2):
+    def spot(first, d):
+        return (d, 0) if first is None else (first, d)
+
+    def sems(h, first, kind):
+        n = 0 if first is None else 1 + first % 4
+        return as_sem.at[h, n, kind], ar_sem.at[h, n, kind]
+
+    def to_next(h, first, d, step, kind, part=None):
+        ref = block(h, *spot(first, d), part)
+        send(ref, ref, *sems(h, first, kind), at(*off(h, *((step, 0) if first is None else (0, step)))))
+
+    def both_ways(h, first):
+        to_next(h, first, 0, 1, 0)
+        to_next(h, first, 0, -1, 1)
+
+    def wait_near(h, first, kind):
+        d = -1 if kind == 0 else 1
+        ref = block(h, *spot(first, d))
+        remote(ref, ref, *sems(h, first, kind), sibling).wait_recv()
+        to_next(h, first, d, -d, 2 + kind, kind)
+
+    def wait_far(h, first):
+        for part in range(2):
+            ref = block(h, *spot(first, 2), part)
+            remote(ref, ref, *sems(h, first, 2 + part), sibling).wait_recv()
+
+    for h in range(2):
+        both_ways(h, None)
+    for h in range(2):
+        both_ways(h, 0)
+    for h in range(2):
+        to_sibling(h, 0, 0)
+    for kind in range(2):
         for h in range(2):
-            ref = block(h, 4 - d, 0)
-            remote(ref, ref, as_sem.at[h, 0, d], ar_sem.at[h, 0, d], sibling).wait_recv()
-            spread_second(h, 4 - d)
-    for first in (0, 3, 1, 2):
-        for d in (1, 3, 2):
+            wait_near(h, None, kind)
+            both_ways(h, 2 * kind - 1)
+            to_sibling(h, 2 * kind - 1, 0)
+    for kind in range(2):
+        for h in range(2):
+            wait_near(h, 0, kind)
+            to_sibling(h, 0, 2 * kind - 1)
+    for h in range(2):
+        wait_far(h, None)
+        both_ways(h, 2)
+        to_sibling(h, 2, 0)
+    for first in (-1, 1, 2):
+        for kind in range(2):
             for h in range(2):
-                ref = block(h, first, 4 - d)
-                remote(ref, ref, as_sem.at[h, 1 + first, d], ar_sem.at[h, 1 + first, d], sibling).wait_recv()
-                to_sibling(h, first, 4 - d)
+                wait_near(h, first, kind)
+                to_sibling(h, first, 2 * kind - 1)
+    for first in (0, -1, 1, 2):
+        for h in range(2):
+            wait_far(h, first)
+            to_sibling(h, first, 2)
     for n in range(16):
         for h in range(2):
             px, py = off(h, n // 4, n % 4)
@@ -200,8 +257,7 @@
 
     def home(h, first, second):
         px, py = off(h, first, second)
-        px, py = (x + px) % NX, (y + py) % NY
-        return px // 2, py * 2 + px % 2
+        return xhs[px], planes[px][py][0]
 
     for d in (2, 1, 3):
         for h in range(2):
@@ -215,11 +271,18 @@
         both = lax.dot_general(
             tk[q].reshape(ROWS, QF), dcat[...], (((0,), (0,)), ((), ())), preferred_element_type=F32
         ).astype(BF)
-        gg_ref[0, pl.ds(q * QF, QF), :] = both[:, :HID]
-        gu_ref[0, pl.ds(q * QF, QF), :] = both[:, HID:]
+        gg[pl.ds(q * QF, QF), :] = both[:, :HID]
+        gu[pl.ds(q * QF, QF), :] = both[:, HID:]
     hid_t = hid[...].T
     for q in range(NQ):
-        gd_ref[0, :, pl.ds(q * QF, QF)] = dot(hid_t, g[q]).astype(BF)
+        gd[:, pl.ds(q * QF, QF)] = dot(hid_t, g[q]).astype(BF)
+    stores = [
+        pltpu.make_async_copy(gg, gg_hbm.at[0], o_sem.at[0]),
+        pltpu.make_async_copy(gu, gu_hbm.at[0], o_sem.at[1]),
+        pltpu.make_async_copy(gd, gd_hbm.at[0], o_sem.at[2]),
+    ]
+    for copy in stores:
+        copy.start()
 
     for h in range(2):
         s1, r1, s2, r2 = sides[h]
@@ -252,25 +315,65 @@
         place = ((k >= 0) & (k < TOK) & (s == (r // 16) * TOK + k)).astype(F32).astype(BF)
         packed = packed + dot(place, zsum[:, pl.ds(256 * third, 256)])
     sz[...] = packed.astype(BF).reshape(NZ, 16, 256)
-    for d in (8, 7, 9, 6, 10, 5, 11, 4, 12, 3, 13, 2, 14, 1, 15):
-        send(sz.at[(z + d) % NZ], rz.at[d], fs_sem.at[d], fr_sem.at[d], zdev(d))
+    def hand_in(step, d):
+        send(sz.at[zs[d % NZ]], rz.at[-d % NZ], fs_sem.at[-d % NZ], fr_sem.at[-d % NZ], zdev(step))
+
+    def handed(d):
+        remote(sz.at[z], rz.at[d % NZ], fs_sem.at[d % NZ], fr_sem.at[d % NZ], sibling).wait_recv()
+        return rz[d % NZ].astype(F32)
+
+    for far in (8, 7, 6, 5, 3):
+        hand_in(4 - far, -far)
+    for far in (7, 6, 5, 3):
+        hand_in(far - 4, far)
+    for d in (1, -1, 2, -2):
+        hand_in(d, d)
+    for hub, fars in ((4, (3, 5, 6, 7, 8)), (-4, (-3, -5, -6, -7))):
+        ref = sz.at[zs[-hub % NZ]]
+        total = ref[...].astype(F32)
+        for far in fars:
+            total = total + handed(far)
+        ref[...] = total.astype(BF)
+        hand_in(-hub, -hub)
     total = sz[z].astype(F32)
-    for d in range(1, NZ):
-        remote(sz.at[(z + d) % NZ], rz.at[d], fs_sem.at[d], fr_sem.at[d], zdev(d)).wait_recv()
-        total = total + rz[d].astype(F32)
+    for d in (1, -1, 2, -2, 4, -4):
+        total = total + handed(d)
     stage[:, pl.ds(0, 256)] = total
     for third in range(3):
         gx_ref[:, pl.ds(256 * third, 256)] = stage[pl.ds(3 * third, TOK), pl.ds(0, 256)].astype(BF)
 
+    for copy in stores:
+        copy.wait()
     for copy in sends:
         copy.wait_send()
+
+
+def settle(gx_in, gg_in, gu_in, gd_in, gx, gg, gu, gd, bg, bu, bd, in_sem, out_sem):
+    gx[...] = gx_in[...]
+    moves = []
+    for i, (src, via, dst) in enumerate(((gg_in, bg, gg), (gu_in, bu, gu), (gd_in, bd, gd))):
+        half = via.shape[0] // 2
+        for j in range(2):
+            part = pl.ds(j * half, half)
+            moves.append((
+                pltpu.make_async_copy(src.at[0, part], via.at[part], in_sem.at[i, j]),
+                pltpu.make_async_copy(via.at[part], dst.at[0, part], out_sem.at[i, j]),
+            ))
+    for come, _ in moves:
+        come.start()
+    for come, go in moves:
+        come.wait()
+        go.start()
+    for _, go in moves:
+        go.wait()
 
 
 def shards(tokens, out_grad, expert_ids, gate_weights, w_gate, w_up, w_down):
     vmem = pl.BlockSpec(memory_space=pltpu.VMEM)
     anywhere = pl.BlockSpec(memory_space=pl.ANY)
+    smem = pl.BlockSpec(memory_space=pltpu.SMEM)
     dma = pltpu.SemaphoreType.DMA
-    return pl.pallas_call(
+    results = pl.pallas_call(
         kernel,
         out_shape=(
             jax.ShapeDtypeStruct((TOK, QF), BF),
@@ -278,8 +381,8 @@
             jax.ShapeDtypeStruct((1, D, HID), BF),
             jax.ShapeDtypeStruct((1, HID, D), BF),
         ),
-        in_specs=[vmem] * 4 + [anywhere] * 3,
-        out_specs=(vmem,) * 4,
+        in_specs=[vmem] * 2 + [smem] * 2 + [anywhere] * 3,
+        out_specs=(vmem,) + (anywhere,) * 3,
         scratch_shapes=[
             pltpu.VMEM((16, HALF), F32),
             pltpu.VMEM((NZ, 16, HALF), BF),
@@ -307,7 +410,10 @@
             pltpu.VMEM((NZ, 16, 256), BF),
             pltpu.VMEM((NZ, 16, 256), BF),
             pltpu.VMEM((GROUP, QF), BF),
-            dma((3,)),
+            pltpu.VMEM((D, HID), BF),
+            pltpu.VMEM((D, HID), BF),
+            pltpu.VMEM((HID, D), BF),
+            dma((3,)), dma((3,)),
             dma((NZ,)), dma((NZ,)),
             dma((2, 5, 4)), dma((2, 5, 4)),
             dma((2, 16)), dma((2, 16)),
@@ -317,11 +423,25 @@
             dma((NZ,)), dma((NZ,)),
         ],
         compiler_params=pltpu.CompilerParams(
-            collective_id=0, has_side_effects=True, vmem_limit_bytes=48 * 2**20
+            collective_id=0, has_side_effects=True, vmem_limit_bytes=60 * 2**20
         ),
         cost_estimate=pl.CostEstimate(flops=2_400_000_000, bytes_accessed=4_800_000, transcendentals=49152),
         name="moe_backward",
-    )(tokens, out_grad, expert_ids, gate_weights, w_gate, w_up, w_down)
+    )(tokens, out_grad, expert_ids.T, gate_weights.T, w_gate, w_up, w_down)
+    return pl.pallas_call(
+        settle,
+        out_shape=[jax.ShapeDtypeStruct(v.shape, v.dtype) for v in results],
+        in_specs=[vmem] + [anywhere] * 3,
+        out_specs=[vmem] + [anywhere] * 3,
+        scratch_shapes=[
+            pltpu.VMEM((D, HID), BF),
+            pltpu.VMEM((D, HID), BF),
+            pltpu.VMEM((HID, D), BF),
+            dma((3, 2)), dma((3, 2)),
+        ],
+        compiler_params=pltpu.CompilerParams(vmem_limit_bytes=60 * 2**20),
+        name="settle",
+    )(*results)
 
 
 def solution(mesh):

time: 86.2 us -> 76.4 us (0.89)
  local copies, waits for them, and re-layouts: 8.86 us -> 0 us
    unnamed x16 -> x0, local copies, waits for them, and re-layouts: 8.86 us -> none
    pallas_call x1, Pallas kernels: 75.8 us -> 71.3 us  [shards(): pl.pallas_call(kernel, out_shape=(jax.ShapeDtypeStruct((TOK, QF), BF), ja...]
    pallas_call x0 -> x1, Pallas kernels: none -> 3.78 us  [shards(): pl.pallas_call(settle, out_shape=[jax.ShapeDtypeStruct(v.shape, v.dtype)...]
where the time goes in v2:
time: 76.4 us; the launch traced here: 75.7 us
  Pallas kernels  75.1 us (98%)
    pallas_call x1, Pallas kernels, shards(): pl.pallas_call(kernel, out_shape=(jax.ShapeDtypeStruct((TOK, QF), BF), ja...  71.3 us
    pallas_call x1, Pallas kernels, shards(): pl.pallas_call(settle, out_shape=[jax.ShapeDtypeStruct(v.shape, v.dtype)...  3.78 us

profile of v2, /device:TPU:1, one launch (start us, length us, event | category | flops | bytes accessed | tf_op | source)
XLA Modules:
  0.0 75.7 jit_solution(4527527452814822002)
XLA Ops:
  0.6 71.3 %moe_backward.1 = (bf16[3,768]{1,0:T(4,128)(2,1)}, bf16[1,3072,128]{2,1,0:T(8,128)(2,1)}, bf16[1,3072,128]{2,1,0:T(8,128)(2,1)}, bf16[1,128,3072]{2,1,0:T(8,128)(2,1)}) custom-call(bf16[3,768]{1,0:T(4,128)(2,1)} %tok_ref.1, bf16[3,768]{1,0:T(4,128)(2,1)} %dy_ref.1, s32[2,3]{1,0:T(2,128)} %bitcast.2, f32[2,3]{1,0:T(2,128)} %bitcast.3, ...), custom_call_target="tpu_custom_call" | custom-call | flops 2400000000 | bytes 4800000 | tf_op jit(solution)/shard_map/moe_backward/pallas_call | solution.py:376
  71.9 3.8 %settle.1 = (bf16[3,768]{1,0:T(4,128)(2,1)}, bf16[1,3072,128]{2,1,0:T(8,128)(2,1)}, bf16[1,3072,128]{2,1,0:T(8,128)(2,1)}, bf16[1,128,3072]{2,1,0:T(8,128)(2,1)}) custom-call(bf16[3,768]{1,0:T(4,128)(2,1)} %get-tuple-element.8.gx_in, bf16[1,3072,128]{2,1,0:T(8,128)(2,1)} %get-tuple-element.9.gg_in, bf16[1,3072,128]{2,1,0:T(8,128)(2,1)} %get-tuple-element.10.gu_in, ...), custom_call_target="tpu_custom_call" | custom-call | tf_op jit(solution)/shard_map/settle/pallas_call | solution.py:431

commit v3 on v2

--- a/solution.py
+++ b/solution.py
@@ -29,10 +29,10 @@
 
 def kernel(
     tok_ref, dy_ref, ids_ref, gw_ref, wg_hbm, wu_hbm, wd_hbm,
-    gx_ref, gg_hbm, gu_hbm, gd_hbm,
+    gx_ref, gg_ref, gu_ref, gd_ref,
     stage, zb, tk, dy, g, wgu, wgut, wd, wdt, acts, dcat, hid, acc, sbuf, rbuf,
-    sl1, rl1, sr1, rr1, sl2, rl2, sr2, rr2, sz, rz, zsum, gg, gu, gd,
-    w_sem, o_sem, zs_sem, zr_sem, as_sem, ar_sem, ds_sem, dr_sem, es_sem, er_sem,
+    sl1, rl1, sr1, rr1, sl2, rl2, sr2, rr2, sz, rz, zsum, mine,
+    w_sem, zs_sem, zr_sem, as_sem, ar_sem, ds_sem, dr_sem, es_sem, er_sem,
     ps_sem, pr_sem, qs_sem, qr_sem, fs_sem, fr_sem,
 ):
     dp = lax.axis_index("dp")
@@ -62,11 +62,11 @@
         group, quarter = planes[dx % NX][dy_ % NY]
         return quarter, group
 
-    loads = [
-        pltpu.make_async_copy(wg_hbm.at[0], wgu.at[:, pl.ds(0, HID)], w_sem.at[0]),
-        pltpu.make_async_copy(wu_hbm.at[0], wgu.at[:, pl.ds(HID, HID)], w_sem.at[1]),
-        pltpu.make_async_copy(wd_hbm.at[0], wd, w_sem.at[2]),
-    ]
+    loads = [pltpu.make_async_copy(wd_hbm.at[0], wd, w_sem.at[2 * NQ])]
+    for q in range(NQ):
+        for i, ref in enumerate((wg_hbm, wu_hbm)):
+            part = ref.at[0, pl.ds(q * QF, QF)]
+            loads.append(pltpu.make_async_copy(part, wgu.at[q, :, pl.ds(i * HID, HID)], w_sem.at[2 * q + i]))
     for copy in loads:
         copy.start()
 
@@ -127,8 +127,8 @@
     for copy in loads:
         copy.wait()
     for q in range(NQ):
-        wgut[q] = wgu[pl.ds(q * QF, QF), :].T
-        wdt[pl.ds(q * QF, QF), :] = wd[:, pl.ds(q * QF, QF)].T
+        wgut[q] = wgu[q].T
+        wdt[q] = wd[:, pl.ds(q * QF, QF)].T
 
     for d in (1, -1, 2, -2, 3, -3, 5, -5, 6, -6, 7, -7, 8):
         arrived(d)
@@ -216,27 +216,31 @@
         for h in range(2):
             wait_far(h, first)
             to_sibling(h, first, 2)
+    route = dy[mq, :, :, pl.ds(QF, 128)].reshape(ROWS, 128).astype(F32)
+    route_lane = lax.broadcasted_iota(jnp.int32, (ROWS, 128), 1)
+    weight = jnp.sum(jnp.where(route_lane % 4 == ex, route, 0.0), axis=1, keepdims=True)
+
+    def forward(q, fresh):
+        part = dot(tk[q].reshape(ROWS, QF), wgu[q])
+        g[q] = (weight * dy[q, :, :, pl.ds(0, QF)].reshape(ROWS, QF).astype(F32)).astype(BF)
+        back = dot(g[q], wdt[q])
+        if fresh:
+            acts[:, pl.ds(0, 2 * HID)] = part
+            acts[:, pl.ds(2 * HID, HID)] = back
+        else:
+            acts[:, pl.ds(0, 2 * HID)] += part
+            acts[:, pl.ds(2 * HID, HID)] += back
+
+    forward(c, True)
+    forward(2 + c, False)
     for n in range(16):
         for h in range(2):
             px, py = off(h, n // 4, n % 4)
             qx, gy = cell(px, py)
             ref = arrays[h][0].at[qx + 1 - 2 * c, gy]
             remote(ref, ref, ds_sem.at[h, n], dr_sem.at[h, n], sibling).wait_recv()
-
-    route = dy[mq, :, :, pl.ds(QF, 128)].reshape(ROWS, 128).astype(F32)
-    route_lane = lax.broadcasted_iota(jnp.int32, (ROWS, 128), 1)
-    weight = jnp.sum(jnp.where(route_lane % 4 == ex, route, 0.0), axis=1, keepdims=True)
-
-    for q in range(NQ):
-        part = dot(tk[q].reshape(ROWS, QF), wgu[pl.ds(q * QF, QF), :])
-        g[q] = (weight * dy[q, :, :, pl.ds(0, QF)].reshape(ROWS, QF).astype(F32)).astype(BF)
-        back = dot(g[q], wdt[pl.ds(q * QF, QF), :])
-        if q == 0:
-            acts[:, pl.ds(0, 2 * HID)] = part
-            acts[:, pl.ds(2 * HID, HID)] = back
-        else:
-            acts[:, pl.ds(0, 2 * HID)] += part
-            acts[:, pl.ds(2 * HID, HID)] += back
+    forward(1 - c, False)
+    forward(3 - c, False)
     gate, up, dh = acts[:, pl.ds(0, HID)], acts[:, pl.ds(HID, HID)], acts[:, pl.ds(2 * HID, HID)]
     sigma = jax.nn.sigmoid(gate)
     active = gate * sigma
@@ -244,64 +248,61 @@
     dcat[:, pl.ds(0, HID)] = (dh * up * (sigma + active * (1.0 - sigma))).astype(BF)
     dcat[:, pl.ds(HID, HID)] = (dh * active).astype(BF)
 
-    for h in range(2):
-        sbuf[h] = dot(dcat[...], wgut[2 * h + 1 - c]).astype(BF).reshape(NG, GROUP, QF)
-        send(sbuf.at[h], rbuf.at[h], es_sem.at[h], er_sem.at[h], sibling)
-    for h in range(2):
-        acc[h] = dot(dcat[...], wgut[2 * h + c]).reshape(NG, GROUP, QF)
-    for h in range(2):
-        remote(sbuf.at[h], rbuf.at[h], es_sem.at[h], er_sem.at[h], sibling).wait_recv()
-        acc[h] = acc[h] + rbuf[h].astype(F32)
-
     sides = ((sl1, rl1, sl2, rl2), (sr1, rr1, sr2, rr2))
 
     def home(h, first, second):
         px, py = off(h, first, second)
         return xhs[px], planes[px][py][0]
 
-    for d in (2, 1, 3):
-        for h in range(2):
-            s1, r1, _, _ = sides[h]
-            for second in range(4):
-                a, b = home(h, d, second)
-                s1[d, second] = acc[a, b, :, pl.ds(h * HALF, HALF)].astype(BF)
-            send(s1.at[d], r1.at[d], ps_sem.at[h, d], pr_sem.at[h, d], at(*off(h, d, 0)))
+    def both_cores(h, first, second):
+        a, b = home(h, first, second)
+        cols = pl.ds(h * HALF, HALF)
+        return acc[a, b, :, cols] + rbuf[a, b, :, cols].astype(F32)
+
+    def first_line(h, d):
+        s1, r1, _, _ = sides[h]
+        for second in range(4):
+            s1[d, second] = both_cores(h, d, second).astype(BF)
+        send(s1.at[d], r1.at[d], ps_sem.at[h, d], pr_sem.at[h, d], at(*off(h, d, 0)))
+
+    near, far = xh, 1 - xh
+    for i, a in enumerate((far, near)):
+        sbuf[a] = dot(dcat[...], wgut[2 * a + 1 - c]).astype(BF).reshape(NG, GROUP, QF)
+        send(sbuf.at[a], rbuf.at[a], es_sem.at[i], er_sem.at[i], sibling)
+    for i, a in enumerate((far, near)):
+        acc[a] = dot(dcat[...], wgut[2 * a + c]).reshape(NG, GROUP, QF)
+        remote(sbuf.at[a], rbuf.at[a], es_sem.at[i], er_sem.at[i], sibling).wait_recv()
+        if i == 0:
+            first_line(0, 2)
+    for h, d in ((1, 2), (0, 1), (1, 1), (0, 3), (1, 3)):
+        first_line(h, d)
 
     for q in range(NQ):
         both = lax.dot_general(
             tk[q].reshape(ROWS, QF), dcat[...], (((0,), (0,)), ((), ())), preferred_element_type=F32
         ).astype(BF)
-        gg[pl.ds(q * QF, QF), :] = both[:, :HID]
-        gu[pl.ds(q * QF, QF), :] = both[:, HID:]
+        gg_ref[0, pl.ds(q * QF, QF), :] = both[:, :HID]
+        gu_ref[0, pl.ds(q * QF, QF), :] = both[:, HID:]
     hid_t = hid[...].T
     for q in range(NQ):
-        gd[:, pl.ds(q * QF, QF)] = dot(hid_t, g[q]).astype(BF)
-    stores = [
-        pltpu.make_async_copy(gg, gg_hbm.at[0], o_sem.at[0]),
-        pltpu.make_async_copy(gu, gu_hbm.at[0], o_sem.at[1]),
-        pltpu.make_async_copy(gd, gd_hbm.at[0], o_sem.at[2]),
-    ]
-    for copy in stores:
-        copy.start()
+        gd_ref[0, :, pl.ds(q * QF, QF)] = dot(hid_t, g[q]).astype(BF)
 
     for h in range(2):
         s1, r1, s2, r2 = sides[h]
         for d in range(1, 4):
             remote(s1.at[d], r1.at[d], ps_sem.at[h, d], pr_sem.at[h, d], sibling).wait_recv()
         for second in (2, 1, 3, 0):
-            a, b = home(h, 0, second)
-            total = acc[a, b, :, pl.ds(h * HALF, HALF)]
+            total = both_cores(h, 0, second)
             for d in range(1, 4):
                 total = total + r1[d, second].astype(F32)
             if second == 0:
-                acc[a, b, :, pl.ds(h * HALF, HALF)] = total
+                mine[:, pl.ds(h * HALF, HALF)] = total
             else:
                 s2[second] = total.astype(BF)
                 send(s2.at[second], r2.at[second], qs_sem.at[h, second], qr_sem.at[h, second], at(*off(h, 0, second)))
-    a0, b0 = home(0, 0, 0)
     for h in range(2):
         s1, r1, s2, r2 = sides[h]
-        total = acc[a0, b0, :, pl.ds(h * HALF, HALF)]
+        total = mine[:, pl.ds(h * HALF, HALF)]
         for d in range(1, 4):
             remote(s2.at[d], r2.at[d], qs_sem.at[h, d], qr_sem.at[h, d], sibling).wait_recv()
             total = total + r2[d].astype(F32)
@@ -342,30 +343,16 @@
     for third in range(3):
         gx_ref[:, pl.ds(256 * third, 256)] = stage[pl.ds(3 * third, TOK), pl.ds(0, 256)].astype(BF)
 
-    for copy in stores:
-        copy.wait()
     for copy in sends:
         copy.wait_send()
 
 
-def settle(gx_in, gg_in, gu_in, gd_in, gx, gg, gu, gd, bg, bu, bd, in_sem, out_sem):
-    gx[...] = gx_in[...]
-    moves = []
-    for i, (src, via, dst) in enumerate(((gg_in, bg, gg), (gu_in, bu, gu), (gd_in, bd, gd))):
-        half = via.shape[0] // 2
-        for j in range(2):
-            part = pl.ds(j * half, half)
-            moves.append((
-                pltpu.make_async_copy(src.at[0, part], via.at[part], in_sem.at[i, j]),
-                pltpu.make_async_copy(via.at[part], dst.at[0, part], out_sem.at[i, j]),
-            ))
-    for come, _ in moves:
-        come.start()
-    for come, go in moves:
-        come.wait()
-        go.start()
-    for _, go in moves:
-        go.wait()
+def settle(*refs):
+    copies = [pltpu.make_async_copy(refs[i], refs[4 + i], refs[8].at[i]) for i in range(4)]
+    for copy in copies:
+        copy.start()
+    for copy in copies:
+        copy.wait()
 
 
 def shards(tokens, out_grad, expert_ids, gate_weights, w_gate, w_up, w_down):
@@ -376,23 +363,23 @@
     results = pl.pallas_call(
         kernel,
         out_shape=(
-            jax.ShapeDtypeStruct((TOK, QF), BF),
-            jax.ShapeDtypeStruct((1, D, HID), BF),
-            jax.ShapeDtypeStruct((1, D, HID), BF),
-            jax.ShapeDtypeStruct((1, HID, D), BF),
+            pltpu.VMEM((TOK, QF), BF),
+            pltpu.VMEM((1, D, HID), BF),
+            pltpu.VMEM((1, D, HID), BF),
+            pltpu.VMEM((1, HID, D), BF),
         ),
         in_specs=[vmem] * 2 + [smem] * 2 + [anywhere] * 3,
-        out_specs=(vmem,) + (anywhere,) * 3,
+        out_specs=(vmem,) * 4,
         scratch_shapes=[
             pltpu.VMEM((16, HALF), F32),
             pltpu.VMEM((NZ, 16, HALF), BF),
             pltpu.VMEM((NQ, NG, GROUP, QF), BF),
             pltpu.VMEM((NQ, NG, GROUP, YW), BF),
             pltpu.VMEM((NQ, ROWS, QF), BF),
-            pltpu.VMEM((D, 2 * HID), BF),
+            pltpu.VMEM((NQ, QF, 2 * HID), BF),
             pltpu.VMEM((NQ, 2 * HID, QF), BF),
             pltpu.VMEM((HID, D), BF),
-            pltpu.VMEM((D, HID), BF),
+            pltpu.VMEM((NQ, QF, HID), BF),
             pltpu.VMEM((ROWS, 3 * HID), F32),
             pltpu.VMEM((ROWS, 2 * HID), BF),
             pltpu.VMEM((ROWS, HID), BF),
@@ -410,10 +397,8 @@
             pltpu.VMEM((NZ, 16, 256), BF),
             pltpu.VMEM((NZ, 16, 256), BF),
             pltpu.VMEM((GROUP, QF), BF),
-            pltpu.VMEM((D, HID), BF),
-            pltpu.VMEM((D, HID), BF),
-            pltpu.VMEM((HID, D), BF),
-            dma((3,)), dma((3,)),
+            pltpu.VMEM((GROUP, QF), F32),
+            dma((2 * NQ + 1,)),
             dma((NZ,)), dma((NZ,)),
             dma((2, 5, 4)), dma((2, 5, 4)),
             dma((2, 16)), dma((2, 16)),
@@ -423,7 +408,7 @@
             dma((NZ,)), dma((NZ,)),
         ],
         compiler_params=pltpu.CompilerParams(
-            collective_id=0, has_side_effects=True, vmem_limit_bytes=60 * 2**20
+            collective_id=0, has_side_effects=True, vmem_limit_bytes=56 * 2**20
         ),
         cost_estimate=pl.CostEstimate(flops=2_400_000_000, bytes_accessed=4_800_000, transcendentals=49152),
         name="moe_backward",
@@ -431,15 +416,10 @@
     return pl.pallas_call(
         settle,
         out_shape=[jax.ShapeDtypeStruct(v.shape, v.dtype) for v in results],
-        in_specs=[vmem] + [anywhere] * 3,
-        out_specs=[vmem] + [anywhere] * 3,
-        scratch_shapes=[
-            pltpu.VMEM((D, HID), BF),
-            pltpu.VMEM((D, HID), BF),
-            pltpu.VMEM((HID, D), BF),
-            dma((3, 2)), dma((3, 2)),
-        ],
-        compiler_params=pltpu.CompilerParams(vmem_limit_bytes=60 * 2**20),
+        in_specs=[anywhere] * 4,
+        out_specs=[anywhere] * 4,
+        scratch_shapes=[dma((4,))],
+        compiler_params=pltpu.CompilerParams(vmem_limit_bytes=2**20),
         name="settle",
     )(*results)
 

time: 76.4 us -> 73.4 us (0.961)
  Pallas kernels: 75.1 us -> 72.2 us
    pallas_call x1, Pallas kernels: 3.78 us -> 1.44 us  [shards(): pl.pallas_call(settle, out_shape=[jax.ShapeDtypeStruct(v.shape, v.dtype)...]
where the time goes in v3:
time: 73.4 us; the launch traced here: 72.8 us
  Pallas kernels  72.2 us (98%)
    pallas_call x1, Pallas kernels, shards(): pl.pallas_call(kernel, out_shape=(pltpu.VMEM((TOK, QF), BF), pltpu.VMEM((...  70.7 us

profile of v3, /device:TPU:1, one launch (start us, length us, event | category | flops | bytes accessed | tf_op | source)
XLA Modules:
  0.0 72.8 jit_solution(6873161826893642715)
XLA Ops:
  0.6 70.7 %moe_backward.1 = (bf16[3,768]{1,0:T(4,128)(2,1)S(1)}, bf16[1,3072,128]{2,1,0:T(8,128)(2,1)S(1)}, bf16[1,3072,128]{2,1,0:T(8,128)(2,1)S(1)}, bf16[1,128,3072]{2,1,0:T(8,128)(2,1)S(1)}) custom-call(bf16[3,768]{1,0:T(4,128)(2,1)} %tok_ref.1, bf16[3,768]{1,0:T(4,128)(2,1)} %dy_ref.1, s32[2,3]{1,0:T(2,128)} %bitcast.2, f32[2,3]{1,0:T(2,128)} %bitcast.3, ...), custom_call_target="tpu_custom_call" | custom-call | flops 2400000000 | bytes 4800000 | tf_op jit(solution)/shard_map/moe_backward/pallas_call | solution.py:363
  71.4 1.4 %settle.1 = (bf16[3,768]{1,0:T(4,128)(2,1)}, bf16[1,3072,128]{2,1,0:T(8,128)(2,1)}, bf16[1,3072,128]{2,1,0:T(8,128)(2,1)}, bf16[1,128,3072]{2,1,0:T(8,128)(2,1)}) custom-call(bf16[3,768]{1,0:T(4,128)(2,1)S(1)} %get-tuple-element.8.refs_0_, bf16[1,3072,128]{2,1,0:T(8,128)(2,1)S(1)} %get-tuple-element.9.refs_1_, ...), custom_call_target="tpu_custom_call" | custom-call | tf_op jit(solution)/shard_map/settle/pallas_call | solution.py:416

commit v4 on v3

--- a/solution.py
+++ b/solution.py
@@ -17,9 +17,6 @@
 ROWS = NG * GROUP
 HID = 128
 D = NQ * QF
-YW = QF + 128
-WIDE = (QF, YW)
-CUT = (384, 512)
 BF, F32 = jnp.bfloat16, jnp.float32
 
 
@@ -28,11 +25,11 @@
 
 
 def kernel(
-    tok_ref, dy_ref, ids_ref, gw_ref, wg_hbm, wu_hbm, wd_hbm,
+    tok_hbm, dy_hbm, ids_hbm, gw_hbm, wg_hbm, wu_hbm, wd_hbm,
     gx_ref, gg_ref, gu_ref, gd_ref,
-    stage, zb, tk, dy, g, wgu, wgut, wd, wdt, acts, dcat, hid, acc, sbuf, rbuf,
+    tok_ref, dy_ref, ids_ref, gw_ref, stage, zb, tk, dy, rt, g, wgu, wgut, wd, wdt, acts, dcat, hid, acc, sbuf, rbuf,
     sl1, rl1, sr1, rr1, sl2, rl2, sr2, rr2, sz, rz, zsum, mine,
-    w_sem, zs_sem, zr_sem, as_sem, ar_sem, ds_sem, dr_sem, es_sem, er_sem,
+    i_sem, w_sem, zs_sem, zr_sem, rs_sem, rr_sem, as_sem, ar_sem, ds_sem, dr_sem, es_sem, er_sem,
     ps_sem, pr_sem, qs_sem, qr_sem, fs_sem, fr_sem,
 ):
     dp = lax.axis_index("dp")
@@ -62,6 +59,17 @@
         group, quarter = planes[dx % NX][dy_ % NY]
         return quarter, group
 
+    pairs = ((tok_hbm, tok_ref), (dy_hbm, dy_ref), (ids_hbm, ids_ref), (gw_hbm, gw_ref))
+    inputs = [pltpu.make_async_copy(src, dst, i_sem.at[i]) for i, (src, dst) in enumerate(pairs)]
+    for copy in inputs:
+        copy.start()
+
+    barrier = pltpu.get_barrier_semaphore()
+    peers = [zdev(d) for d in PEERS_Z]
+    peers += [at(d, 0) for d in range(1, NX)] + [at(0, d) for d in range(1, NY)] + [sibling]
+    for peer in peers:
+        pl.semaphore_signal(barrier, inc=1, device_id=peer, device_id_type=MESH)
+
     loads = [pltpu.make_async_copy(wd_hbm.at[0], wd, w_sem.at[2 * NQ])]
     for q in range(NQ):
         for i, ref in enumerate((wg_hbm, wu_hbm)):
@@ -70,11 +78,8 @@
     for copy in loads:
         copy.start()
 
-    barrier = pltpu.get_barrier_semaphore()
-    peers = [zdev(d) for d in PEERS_Z]
-    peers += [at(d, 0) for d in range(1, NX)] + [at(0, d) for d in range(1, NY)] + [sibling]
-    for peer in peers:
-        pl.semaphore_signal(barrier, inc=1, device_id=peer, device_id_type=MESH)
+    for copy in inputs:
+        copy.wait()
 
     stage[...] = jnp.zeros_like(stage)
     for i, ref in enumerate((tok_ref, dy_ref)):
@@ -144,7 +149,7 @@
     tk[mq, mg, :, pl.ds(HALF, HALF)] = rows[GROUP : 2 * GROUP]
     dy[mq, mg, :, pl.ds(0, HALF)] = rows[2 * GROUP : 3 * GROUP]
     dy[mq, mg, :, pl.ds(HALF, HALF)] = rows[3 * GROUP : 4 * GROUP]
-    dy[mq, mg, :, pl.ds(QF, 128)] = rows[4 * GROUP : 5 * GROUP, 0:128]
+    rt[mg] = rows[4 * GROUP : 5 * GROUP, 0:128]
 
     arrays = ((tk, 0), (dy, 1))
 
@@ -155,11 +160,13 @@
         q_, g_ = cell(*off(h, first, second))
         if part is None:
             return arrays[h][0].at[q_, g_]
-        return arrays[h][0].at[q_, g_, :, pl.ds(*((0, CUT[h]) if part == 0 else (CUT[h], WIDE[h] - CUT[h])))]
-
-    def to_sibling(h, first, second):
-        ref = block(h, first, second)
+        return arrays[h][0].at[q_, g_, :, pl.ds(part * HALF, HALF)]
+
+    def to_sibling(h, first, second, part=None):
+        ref = block(h, first, second, part)
         n = (first % 4) * 4 + second % 4
+        if part == 1:
+            n = 20 if second == 0 else 16 + first % 4
         send(ref, ref, ds_sem.at[h, n], dr_sem.at[h, n], sibling)
 
     def spot(first, d):
@@ -187,9 +194,16 @@
         for part in range(2):
             ref = block(h, *spot(first, 2), part)
             remote(ref, ref, *sems(h, first, 2 + part), sibling).wait_recv()
+            to_sibling(h, *spot(first, 2), part)
 
     for h in range(2):
         both_ways(h, None)
+
+    def group(dx, dy_):
+        return rt.at[planes[dx % NX][dy_ % NY][0]]
+
+    for d in range(1, 4):
+        send(group(0, 0), group(0, 0), rs_sem.at[3 + d], rr_sem.at[3 + d], at(0, d))
     for h in range(2):
         both_ways(h, 0)
     for h in range(2):
@@ -203,10 +217,14 @@
         for h in range(2):
             wait_near(h, 0, kind)
             to_sibling(h, 0, 2 * kind - 1)
+    for d in range(4):
+        ref = group(0, d)
+        if d > 0:
+            remote(ref, ref, rs_sem.at[7 - d], rr_sem.at[7 - d], sibling).wait_recv()
+        send(ref, ref, rs_sem.at[d], rr_sem.at[d], at(1 if d < 2 else -1, 0))
     for h in range(2):
         wait_far(h, None)
         both_ways(h, 2)
-        to_sibling(h, 2, 0)
     for first in (-1, 1, 2):
         for kind in range(2):
             for h in range(2):
@@ -215,14 +233,16 @@
     for first in (0, -1, 1, 2):
         for h in range(2):
             wait_far(h, first)
-            to_sibling(h, first, 2)
-    route = dy[mq, :, :, pl.ds(QF, 128)].reshape(ROWS, 128).astype(F32)
+    for d in range(4):
+        ref = group(1, d)
+        remote(ref, ref, rs_sem.at[d], rr_sem.at[d], sibling).wait_recv()
+    route = rt[...].reshape(ROWS, 128).astype(F32)
     route_lane = lax.broadcasted_iota(jnp.int32, (ROWS, 128), 1)
     weight = jnp.sum(jnp.where(route_lane % 4 == ex, route, 0.0), axis=1, keepdims=True)
 
     def forward(q, fresh):
         part = dot(tk[q].reshape(ROWS, QF), wgu[q])
-        g[q] = (weight * dy[q, :, :, pl.ds(0, QF)].reshape(ROWS, QF).astype(F32)).astype(BF)
+        g[q] = (weight * dy[q].reshape(ROWS, QF).astype(F32)).astype(BF)
         back = dot(g[q], wdt[q])
         if fresh:
             acts[:, pl.ds(0, 2 * HID)] = part
@@ -233,11 +253,13 @@
 
     forward(c, True)
     forward(2 + c, False)
-    for n in range(16):
+    for n in range(21):
         for h in range(2):
-            px, py = off(h, n // 4, n % 4)
-            qx, gy = cell(px, py)
-            ref = arrays[h][0].at[qx + 1 - 2 * c, gy]
+            first, second = (n // 4, n % 4) if n < 16 else (2, 0) if n == 20 else (n - 16, 2)
+            quarter, row = cell(*off(h, first, second))
+            ref = arrays[h][0].at[quarter + 1 - 2 * c, row]
+            if n < 16 and n % 4 == 2 or n == 8 or n >= 16:
+                ref = ref.at[:, pl.ds(HALF if n >= 16 else 0, HALF)]
             remote(ref, ref, ds_sem.at[h, n], dr_sem.at[h, n], sibling).wait_recv()
     forward(1 - c, False)
     forward(3 - c, False)
@@ -259,41 +281,49 @@
         cols = pl.ds(h * HALF, HALF)
         return acc[a, b, :, cols] + rbuf[a, b, :, cols].astype(F32)
 
-    def first_line(h, d):
+    def first_axis(h, d, second):
         s1, r1, _, _ = sides[h]
-        for second in range(4):
-            s1[d, second] = both_cores(h, d, second).astype(BF)
-        send(s1.at[d], r1.at[d], ps_sem.at[h, d], pr_sem.at[h, d], at(*off(h, d, 0)))
+        s1[d, second] = both_cores(h, d, second).astype(BF)
+        sem = ps_sem.at[h, d, second], pr_sem.at[h, d, second]
+        send(s1.at[d, second], r1.at[d, second], *sem, at(*off(h, d, 0)))
 
     near, far = xh, 1 - xh
+
+    def piece(ref, i, h):
+        return ref.at[(far, near)[i], :, :, pl.ds(h * HALF, HALF)]
+
     for i, a in enumerate((far, near)):
         sbuf[a] = dot(dcat[...], wgut[2 * a + 1 - c]).astype(BF).reshape(NG, GROUP, QF)
-        send(sbuf.at[a], rbuf.at[a], es_sem.at[i], er_sem.at[i], sibling)
-    for i, a in enumerate((far, near)):
-        acc[a] = dot(dcat[...], wgut[2 * a + c]).reshape(NG, GROUP, QF)
-        remote(sbuf.at[a], rbuf.at[a], es_sem.at[i], er_sem.at[i], sibling).wait_recv()
-        if i == 0:
-            first_line(0, 2)
-    for h, d in ((1, 2), (0, 1), (1, 1), (0, 3), (1, 3)):
-        first_line(h, d)
-
-    for q in range(NQ):
-        both = lax.dot_general(
-            tk[q].reshape(ROWS, QF), dcat[...], (((0,), (0,)), ((), ())), preferred_element_type=F32
-        ).astype(BF)
-        gg_ref[0, pl.ds(q * QF, QF), :] = both[:, :HID]
-        gu_ref[0, pl.ds(q * QF, QF), :] = both[:, HID:]
-    hid_t = hid[...].T
-    for q in range(NQ):
-        gd_ref[0, :, pl.ds(q * QF, QF)] = dot(hid_t, g[q]).astype(BF)
-
-    for h in range(2):
-        s1, r1, s2, r2 = sides[h]
-        for d in range(1, 4):
-            remote(s1.at[d], r1.at[d], ps_sem.at[h, d], pr_sem.at[h, d], sibling).wait_recv()
-        for second in (2, 1, 3, 0):
+        for h in (1, 0):
+            send(piece(sbuf, i, h), piece(rbuf, i, h), es_sem.at[i, h], er_sem.at[i, h], sibling)
+
+    def from_sibling(i, h):
+        remote(piece(sbuf, i, h), piece(rbuf, i, h), es_sem.at[i, h], er_sem.at[i, h], sibling).wait_recv()
+
+    acc[far] = dot(dcat[...], wgut[2 * far + c]).reshape(NG, GROUP, QF)
+    from_sibling(0, 1)
+    for d in (2, 1, 3):
+        first_axis(1, d, 2)
+    from_sibling(0, 0)
+    for second in (2, 1, 3, 0):
+        first_axis(0, 2, second)
+    acc[near] = dot(dcat[...], wgut[2 * near + c]).reshape(NG, GROUP, QF)
+    for h in (1, 0):
+        from_sibling(1, h)
+    for second in (2, 1, 3, 0):
+        for d in (1, 3):
+            first_axis(0, d, second)
+        if second != 2:
+            for d in (2, 1, 3):
+                first_axis(1, d, second)
+
+    for second in (2, 1, 3, 0):
+        for h in range(2):
+            s1, r1, s2, r2 = sides[h]
             total = both_cores(h, 0, second)
             for d in range(1, 4):
+                sem = ps_sem.at[h, d, second], pr_sem.at[h, d, second]
+                remote(s1.at[d, second], r1.at[d, second], *sem, sibling).wait_recv()
                 total = total + r1[d, second].astype(F32)
             if second == 0:
                 mine[:, pl.ds(h * HALF, HALF)] = total
@@ -329,6 +359,13 @@
         hand_in(far - 4, far)
     for d in (1, -1, 2, -2):
         hand_in(d, d)
+    for q in range(NQ):
+        both = lax.dot_general(
+            tk[q].reshape(ROWS, QF), dcat[...], (((0,), (0,)), ((), ())), preferred_element_type=F32
+        ).astype(BF)
+        gg_ref[0, pl.ds(q * QF, QF), :] = both[:, :HID]
+        gu_ref[0, pl.ds(q * QF, QF), :] = both[:, HID:]
+
     for hub, fars in ((4, (3, 5, 6, 7, 8)), (-4, (-3, -5, -6, -7))):
         ref = sz.at[zs[-hub % NZ]]
         total = ref[...].astype(F32)
@@ -336,6 +373,10 @@
             total = total + handed(far)
         ref[...] = total.astype(BF)
         hand_in(-hub, -hub)
+    hid_t = hid[...].T
+    for q in range(NQ):
+        gd_ref[0, :, pl.ds(q * QF, QF)] = dot(hid_t, g[q]).astype(BF)
+
     total = sz[z].astype(F32)
     for d in (1, -1, 2, -2, 4, -4):
         total = total + handed(d)
@@ -358,7 +399,6 @@
 def shards(tokens, out_grad, expert_ids, gate_weights, w_gate, w_up, w_down):
     vmem = pl.BlockSpec(memory_space=pltpu.VMEM)
     anywhere = pl.BlockSpec(memory_space=pl.ANY)
-    smem = pl.BlockSpec(memory_space=pltpu.SMEM)
     dma = pltpu.SemaphoreType.DMA
     results = pl.pallas_call(
         kernel,
@@ -368,13 +408,18 @@
             pltpu.VMEM((1, D, HID), BF),
             pltpu.VMEM((1, HID, D), BF),
         ),
-        in_specs=[vmem] * 2 + [smem] * 2 + [anywhere] * 3,
+        in_specs=[anywhere] * 7,
         out_specs=(vmem,) * 4,
         scratch_shapes=[
+            pltpu.VMEM((TOK, QF), BF),
+            pltpu.VMEM((TOK, QF), BF),
+            pltpu.SMEM((2, TOK), jnp.int32),
+            pltpu.SMEM((2, TOK), F32),
             pltpu.VMEM((16, HALF), F32),
             pltpu.VMEM((NZ, 16, HALF), BF),
             pltpu.VMEM((NQ, NG, GROUP, QF), BF),
-            pltpu.VMEM((NQ, NG, GROUP, YW), BF),
+            pltpu.VMEM((NQ, NG, GROUP, QF), BF),
+            pltpu.VMEM((NG, GROUP, 128), BF),
             pltpu.VMEM((NQ, ROWS, QF), BF),
             pltpu.VMEM((NQ, QF, 2 * HID), BF),
             pltpu.VMEM((NQ, 2 * HID, QF), BF),
@@ -398,12 +443,14 @@
             pltpu.VMEM((NZ, 16, 256), BF),
             pltpu.VMEM((GROUP, QF), BF),
             pltpu.VMEM((GROUP, QF), F32),
+            dma((4,)),
             dma((2 * NQ + 1,)),
             dma((NZ,)), dma((NZ,)),
+            dma((7,)), dma((7,)),
             dma((2, 5, 4)), dma((2, 5, 4)),
-            dma((2, 16)), dma((2, 16)),
-            dma((2,)), dma((2,)),
-            dma((2, 4)), dma((2, 4)),
+            dma((2, 21)), dma((2, 21)),
+            dma((2, 2)), dma((2, 2)),
+            dma((2, 4, 4)), dma((2, 4, 4)),
             dma((2, 4)), dma((2, 4)),
             dma((NZ,)), dma((NZ,)),
         ],

time: 73.4 us -> 71.1 us (0.969)
  Pallas kernels: 72.2 us -> 69.3 us
    pallas_call x1, Pallas kernels: 70.7 us -> 67.9 us  [shards(): pl.pallas_call(kernel, out_shape=(pltpu.VMEM((TOK, QF), BF), pltpu.VMEM((...]
where the time goes in v4:
time: 71.1 us; the launch traced here: 69.9 us
  Pallas kernels  69.3 us (97%)
    pallas_call x1, Pallas kernels, shards(): pl.pallas_call(kernel, out_shape=(pltpu.VMEM((TOK, QF), BF), pltpu.VMEM((...  67.9 us
    pallas_call x1, Pallas kernels, shards(): pl.pallas_call(settle, out_shape=[jax.ShapeDtypeStruct(v.shape, v.dtype)...  1.44 us

profile of v4, /device:TPU:1, one launch (start us, length us, event | category | flops | bytes accessed | tf_op | source)
XLA Modules:
  0.0 69.9 jit_solution(9062506581171722)
XLA Ops:
  0.6 67.9 %moe_backward.1 = (bf16[3,768]{1,0:T(4,128)(2,1)S(1)}, bf16[1,3072,128]{2,1,0:T(8,128)(2,1)S(1)}, bf16[1,3072,128]{2,1,0:T(8,128)(2,1)S(1)}, bf16[1,128,3072]{2,1,0:T(8,128)(2,1)S(1)}) custom-call(bf16[3,768]{1,0:T(4,128)(2,1)} %tok_hbm.1, bf16[3,768]{1,0:T(4,128)(2,1)} %dy_hbm.1, s32[2,3]{1,0:T(2,128)} %bitcast.2, f32[2,3]{1,0:T(2,128)} %bitcast.3, ...), custom_call_target="tpu_custom_call" | custom-call | flops 2400000000 | bytes 4800000 | tf_op jit(solution)/shard_map/moe_backward/pallas_call | solution.py:403
  68.5 1.4 %settle.1 = (bf16[3,768]{1,0:T(4,128)(2,1)}, bf16[1,3072,128]{2,1,0:T(8,128)(2,1)}, bf16[1,3072,128]{2,1,0:T(8,128)(2,1)}, bf16[1,128,3072]{2,1,0:T(8,128)(2,1)}) custom-call(bf16[3,768]{1,0:T(4,128)(2,1)S(1)} %get-tuple-element.8.refs_0_, bf16[1,3072,128]{2,1,0:T(8,128)(2,1)S(1)} %get-tuple-element.9.refs_1_, ...), custom_call_target="tpu_custom_call" | custom-call | tf_op jit(solution)/shard_map/settle/pallas_call | solution.py:463

commit v5 on v4

--- a/solution.py
+++ b/solution.py
@@ -7,7 +7,7 @@
 
 MESH = pl.DeviceIdType.MESH
 NX, NY, NZ = 4, 4, 16
-PEERS_Z = (1, 2, 3, 4, -1, -2, -3, -4)
+PEERS_Z = (4, -4, 3, -3, 2, -2, 1, -1)
 TOK = 3
 QF = 768
 NQ = 4
@@ -41,7 +41,7 @@
 
     xs = [x] + [rem(x + d, NX) for d in range(1, NX)]
     ys = [y] + [rem(y + d, NY) for d in range(1, NY)]
-    zs = [z] + [rem(z + d, NZ) for d in range(1, NZ)]
+    zs = [z] + [rem(z + NZ + (1 - 2 * c) * d, NZ) for d in range(1, NZ)]
     xhs, xls = [div(v, 2) for v in xs], [rem(v, 2) for v in xs]
     planes = [[(ys[j] * 2 + xls[i], xhs[i] * 2 + c) for j in range(NY)] for i in range(NX)]
     here = planes[0][0][0] * NZ
@@ -116,7 +116,7 @@
         ref = zb.at[zs[origin % NZ]]
         send(ref, ref, zs_sem.at[d % NZ], zr_sem.at[d % NZ], zdev(step))
 
-    for d in (4, -4, 2, -2, 1, -1):
+    for d in (4, -4, 3, -3, 2, -2, 1, -1):
         pass_on(0, d, d)
 
     def arrived(d):
@@ -124,10 +124,10 @@
         remote(ref, ref, zs_sem.at[d % NZ], zr_sem.at[d % NZ], sibling).wait_recv()
 
     arrived(4)
-    for step in (4, 3, 2, 1, -1):
+    for step in (4, 3, 2, 1):
         pass_on(-4, step, 4 + step)
     arrived(-4)
-    for step in (-3, -2, -1, 1):
+    for step in (-3, -2, -1):
         pass_on(4, step, step - 4)
     for copy in loads:
         copy.wait()
@@ -253,16 +253,30 @@
 
     forward(c, True)
     forward(2 + c, False)
-    for n in range(21):
+    def from_other_core(side, pair, j):
+        dx = ((0, 1 + 2 * xl), (2, 3 - 2 * xl))[side][pair]
+        quarter = 2 * (xh, 1 - xh)[side] + 1 - c
+        row = ys[j] * 2 + (xl, 1 - xl)[pair]
         for h in range(2):
-            first, second = (n // 4, n % 4) if n < 16 else (2, 0) if n == 20 else (n - 16, 2)
-            quarter, row = cell(*off(h, first, second))
-            ref = arrays[h][0].at[quarter + 1 - 2 * c, row]
-            if n < 16 and n % 4 == 2 or n == 8 or n >= 16:
-                ref = ref.at[:, pl.ds(HALF if n >= 16 else 0, HALF)]
-            remote(ref, ref, ds_sem.at[h, n], dr_sem.at[h, n], sibling).wait_recv()
-    forward(1 - c, False)
-    forward(3 - c, False)
+            ref = arrays[h][0].at[quarter, row]
+            n = dx * 4 + j if h == 0 else j * 4 + dx
+            opposite_x, same_x = side == 1 and pair == 0, side == 0 and pair == 0
+            second_half = None
+            if h == 0:
+                second_half = 16 + dx if j == 2 else 20 if opposite_x and j == 0 else None
+            else:
+                second_half = 16 + j if opposite_x else 20 if same_x and j == 2 else None
+            pieces = [(n, ref)]
+            if second_half is not None:
+                pieces = [(n, ref.at[:, pl.ds(0, HALF)]), (second_half, ref.at[:, pl.ds(HALF, HALF)])]
+            for m, part in pieces:
+                remote(part, part, ds_sem.at[h, m], dr_sem.at[h, m], sibling).wait_recv()
+
+    for side in range(2):
+        for pair in range(2):
+            for j in range(4):
+                from_other_core(side, pair, j)
+        forward(2 * (xh, 1 - xh)[side] + 1 - c, False)
     gate, up, dh = acts[:, pl.ds(0, HID)], acts[:, pl.ds(HID, HID)], acts[:, pl.ds(2 * HID, HID)]
     sigma = jax.nn.sigmoid(gate)
     active = gate * sigma
@@ -293,8 +307,9 @@
         return ref.at[(far, near)[i], :, :, pl.ds(h * HALF, HALF)]
 
     for i, a in enumerate((far, near)):
-        sbuf[a] = dot(dcat[...], wgut[2 * a + 1 - c]).astype(BF).reshape(NG, GROUP, QF)
         for h in (1, 0):
+            cols = pl.ds(h * HALF, HALF)
+            sbuf[a, :, :, cols] = dot(dcat[...], wgut[2 * a + 1 - c, :, cols]).astype(BF).reshape(NG, GROUP, HALF)
             send(piece(sbuf, i, h), piece(rbuf, i, h), es_sem.at[i, h], er_sem.at[i, h], sibling)
 
     def from_sibling(i, h):
@@ -353,11 +368,11 @@
         remote(sz.at[z], rz.at[d % NZ], fs_sem.at[d % NZ], fr_sem.at[d % NZ], sibling).wait_recv()
         return rz[d % NZ].astype(F32)
 
-    for far in (8, 7, 6, 5, 3):
-        hand_in(4 - far, -far)
-    for far in (7, 6, 5, 3):
-        hand_in(far - 4, far)
-    for d in (1, -1, 2, -2):
+    for away in (8, 7, 6, 5):
+        hand_in(4 - away, -away)
+    for away in (7, 6, 5):
+        hand_in(away - 4, away)
+    for d in (3, -3, 2, -2, 1, -1):
         hand_in(d, d)
     for q in range(NQ):
         both = lax.dot_general(
@@ -366,7 +381,7 @@
         gg_ref[0, pl.ds(q * QF, QF), :] = both[:, :HID]
         gu_ref[0, pl.ds(q * QF, QF), :] = both[:, HID:]
 
-    for hub, fars in ((4, (3, 5, 6, 7, 8)), (-4, (-3, -5, -6, -7))):
+    for hub, fars in ((4, (5, 6, 7, 8)), (-4, (-5, -6, -7))):
         ref = sz.at[zs[-hub % NZ]]
         total = ref[...].astype(F32)
         for far in fars:
@@ -378,7 +393,7 @@
         gd_ref[0, :, pl.ds(q * QF, QF)] = dot(hid_t, g[q]).astype(BF)
 
     total = sz[z].astype(F32)
-    for d in (1, -1, 2, -2, 4, -4):
+    for d in (1, -1, 2, -2, 3, -3, 4, -4):
         total = total + handed(d)
     stage[:, pl.ds(0, 256)] = total
     for third in range(3):

time: 71.1 us -> 70.8 us (level); the launches traced: 69.9 us -> 70.4 us
  no operation moved by 1% of the time
where the time goes in v5:
time: 70.8 us; the launch traced here: 70.4 us
  Pallas kernels  69.8 us (99%)
    pallas_call x1, Pallas kernels, shards(): pl.pallas_call(kernel, out_shape=(pltpu.VMEM((TOK, QF), BF), pltpu.VMEM((...  68.3 us
    pallas_call x1, Pallas kernels, shards(): pl.pallas_call(settle, out_shape=[jax.ShapeDtypeStruct(v.shape, v.dtype)...  1.44 us

profile of v5, /device:TPU:1, one launch (start us, length us, event | category | flops | bytes accessed | tf_op | source)
XLA Modules:
  0.0 70.4 jit_solution(11972572099122586319)
XLA Ops:
  0.6 68.3 %moe_backward.1 = (bf16[3,768]{1,0:T(4,128)(2,1)S(1)}, bf16[1,3072,128]{2,1,0:T(8,128)(2,1)S(1)}, bf16[1,3072,128]{2,1,0:T(8,128)(2,1)S(1)}, bf16[1,128,3072]{2,1,0:T(8,128)(2,1)S(1)}) custom-call(bf16[3,768]{1,0:T(4,128)(2,1)} %tok_hbm.1, bf16[3,768]{1,0:T(4,128)(2,1)} %dy_hbm.1, s32[2,3]{1,0:T(2,128)} %bitcast.2, f32[2,3]{1,0:T(2,128)} %bitcast.3, ...), custom_call_target="tpu_custom_call" | custom-call | flops 2400000000 | bytes 4800000 | tf_op jit(solution)/shard_map/moe_backward/pallas_call | solution.py:418
  69.0 1.4 %settle.1 = (bf16[3,768]{1,0:T(4,128)(2,1)}, bf16[1,3072,128]{2,1,0:T(8,128)(2,1)}, bf16[1,3072,128]{2,1,0:T(8,128)(2,1)}, bf16[1,128,3072]{2,1,0:T(8,128)(2,1)}) custom-call(bf16[3,768]{1,0:T(4,128)(2,1)S(1)} %get-tuple-element.8.refs_0_, bf16[1,3072,128]{2,1,0:T(8,128)(2,1)S(1)} %get-tuple-element.9.refs_1_, ...), custom_call_target="tpu_custom_call" | custom-call | tf_op jit(solution)/shard_map/settle/pallas_call | solution.py:478

commit v6 on v5

--- a/solution.py
+++ b/solution.py
@@ -69,14 +69,6 @@
     peers += [at(d, 0) for d in range(1, NX)] + [at(0, d) for d in range(1, NY)] + [sibling]
     for peer in peers:
         pl.semaphore_signal(barrier, inc=1, device_id=peer, device_id_type=MESH)
-
-    loads = [pltpu.make_async_copy(wd_hbm.at[0], wd, w_sem.at[2 * NQ])]
-    for q in range(NQ):
-        for i, ref in enumerate((wg_hbm, wu_hbm)):
-            part = ref.at[0, pl.ds(q * QF, QF)]
-            loads.append(pltpu.make_async_copy(part, wgu.at[q, :, pl.ds(i * HID, HID)], w_sem.at[2 * q + i]))
-    for copy in loads:
-        copy.start()
 
     for copy in inputs:
         copy.wait()
@@ -118,6 +110,14 @@
 
     for d in (4, -4, 3, -3, 2, -2, 1, -1):
         pass_on(0, d, d)
+
+    loads = [pltpu.make_async_copy(wd_hbm.at[0], wd, w_sem.at[2 * NQ])]
+    for q in range(NQ):
+        for i, ref in enumerate((wg_hbm, wu_hbm)):
+            part = ref.at[0, pl.ds(q * QF, QF)]
+            loads.append(pltpu.make_async_copy(part, wgu.at[q, :, pl.ds(i * HID, HID)], w_sem.at[2 * q + i]))
+    for copy in loads:
+        copy.start()
 
     def arrived(d):
         ref = zb.at[zs[-d % NZ]]

time: 70.8 us -> 70.8 us (level)
  no operation moved by 1% of the time
where the time goes in v6:
time: 70.8 us; the launch traced here: 70.4 us
  Pallas kernels  69.8 us (99%)
    pallas_call x1, Pallas kernels, shards(): pl.pallas_call(kernel, out_shape=(pltpu.VMEM((TOK, QF), BF), pltpu.VMEM((...  68.3 us
    pallas_call x1, Pallas kernels, shards(): pl.pallas_call(settle, out_shape=[jax.ShapeDtypeStruct(v.shape, v.dtype)...  1.44 us

profile of v6, /device:TPU:1, one launch (start us, length us, event | category | flops | bytes accessed | tf_op | source)
XLA Modules:
  0.0 70.4 jit_solution(11186811912719365382)
XLA Ops:
  0.6 68.3 %moe_backward.1 = (bf16[3,768]{1,0:T(4,128)(2,1)S(1)}, bf16[1,3072,128]{2,1,0:T(8,128)(2,1)S(1)}, bf16[1,3072,128]{2,1,0:T(8,128)(2,1)S(1)}, bf16[1,128,3072]{2,1,0:T(8,128)(2,1)S(1)}) custom-call(bf16[3,768]{1,0:T(4,128)(2,1)} %tok_hbm.1, bf16[3,768]{1,0:T(4,128)(2,1)} %dy_hbm.1, s32[2,3]{1,0:T(2,128)} %bitcast.2, f32[2,3]{1,0:T(2,128)} %bitcast.3, ...), custom_call_target="tpu_custom_call" | custom-call | flops 2400000000 | bytes 4800000 | tf_op jit(solution)/shard_map/moe_backward/pallas_call | solution.py:418
  69.0 1.4 %settle.1 = (bf16[3,768]{1,0:T(4,128)(2,1)}, bf16[1,3072,128]{2,1,0:T(8,128)(2,1)}, bf16[1,3072,128]{2,1,0:T(8,128)(2,1)}, bf16[1,128,3072]{2,1,0:T(8,128)(2,1)}) custom-call(bf16[3,768]{1,0:T(4,128)(2,1)S(1)} %get-tuple-element.8.refs_0_, bf16[1,3072,128]{2,1,0:T(8,128)(2,1)S(1)} %get-tuple-element.9.refs_1_, ...), custom_call_target="tpu_custom_call" | custom-call | tf_op jit(solution)/shard_map/settle/pallas_call | solution.py:478
